TPU v7x, 32 devices: a whole 2x2x4 slice. The times are simulated.
32 devices in a mesh: wide: 8 (over z, y), narrow: 4 (over x, core).
Axes of the slice: x: 2, y: 2, z: 4, core: 2. Of those that a mesh axis runs over, the one named last changes fastest.
Arguments:
- items: bfloat16 [16384, 256], P(('wide', 'narrow')), may hold values from -6 to 6
- tile1_values: bfloat16 [384, 128, 128], P(('wide', 'narrow')), may hold values from -0.3125 to 0.3125
- tile1_source: int32 [384], P(('wide', 'narrow')), may hold values from 0 to 3
- tile1_owner: int32 [384, 1], P(('wide', 'narrow')), may hold values from 0 to 7; in each aligned block of 12 rows (0 to 11, 12 to 23, ...) at most 2 rows name the same one
- tile1_slot: int32 [384], P(('wide', 'narrow')), may hold values from 0 to 3
- tile2_values: bfloat16 [384, 128, 128], P(('wide', 'narrow')), may hold values from -0.3125 to 0.3125
- tile2_source: int32 [384], P(('wide', 'narrow')), may hold values from 0 to 3
- tile2_owner: int32 [384, 1], P(('wide', 'narrow')), may hold values from 0 to 7; in each aligned block of 12 rows (0 to 11, 12 to 23, ...) at most 2 rows name the same one
- tile2_slot: int32 [384], P(('wide', 'narrow')), may hold values from 0 to 15
- weight: bfloat16 [256, 256], replicated, may hold values from -0.375 to 0.375
- bundle_degree: int32 [16384], P(('wide', 'narrow')), may hold values from 1 to 4
- user_degree: int32 [16384], P('wide'), may hold values from 1 to 4
- cotangent: bfloat16 [16384, 256], P('wide'), may hold values from -6 to 6
Outputs:
- user_out: bfloat16 [16384, 256], P('wide')
- grad_weight: float32 [256, 256], replicated
- grad_bundle: bfloat16 [16384, 256], P(('wide', 'narrow'))
Inputs may be any that keep to these rules, and one draw needn't show every extreme that they name: `tile1_owner`: among the 12 tiles of one device, at most 2 name the same owner, a bound that some block reaches. `tile2_owner`: among the 12 tiles of one device, at most 2 name the same owner, a bound that some block reaches.
All inputs are finite; a program needn't handle non-finite values.
Results may differ from a plain program's by a relative error of at most 0.0073.
Values may be sent and summed in bfloat16 or wider, within the bound.
A program may use at most 128 MiB of HBM per device.

v0:
```python
import jax
import jax.numpy as jnp
from jax import lax
from jax.sharding import PartitionSpec as P

F = 256
TILE = 128
CAP = 2


def placing(owner_col, width):
    owner = owner_col[:, 0]
    table = (owner[:, None] == jnp.arange(width, dtype=jnp.int32)[None, :]).astype(jnp.int32)
    rank = jnp.sum(jnp.cumsum(table, axis=0) * table, axis=1) - 1
    return owner * CAP + rank


def bucketed(terms, slots, where, width):
    buffer = jnp.zeros((width * CAP, TILE, F), jnp.bfloat16).at[where].set(terms)
    labels = jnp.full((width * CAP,), -1, jnp.int32).at[where].set(slots)
    return (buffer.reshape(width, CAP, TILE, F), labels.reshape(width, CAP))


def collect(received, labels, count):
    flat = received.reshape(-1, TILE * F)
    table = (labels.reshape(-1)[None, :] == jnp.arange(count, dtype=jnp.int32)[:, None]).astype(
        jnp.bfloat16
    )
    return jnp.dot(table, flat, preferred_element_type=jnp.float32).reshape(count * TILE, F)


def local(
    items,
    tile1_values,
    tile1_source,
    tile1_owner,
    tile1_slot,
    tile2_values,
    tile2_source,
    tile2_owner,
    tile2_slot,
    weight,
    bundle_degree,
    user_degree,
    cotangent,
):
    width = lax.axis_size("wide")
    bb_count = bundle_degree.shape[0] // TILE
    group = user_degree.shape[0] // TILE
    item_blocks = items.reshape(-1, TILE, F)
    term1 = jnp.einsum(
        "tij,tjf->tif", tile1_values, item_blocks[tile1_source], preferred_element_type=jnp.float32
    ).astype(jnp.bfloat16)
    where1 = placing(tile1_owner, width)
    buffer1, labels1 = bucketed(term1, tile1_slot, where1, width)
    got1, got_labels1 = (
        lax.all_to_all(buffer1, "wide", split_axis=0, concat_axis=0, tiled=True),
        lax.all_to_all(labels1, "wide", split_axis=0, concat_axis=0, tiled=True),
    )
    summed = collect(got1, got_labels1, bb_count)
    bundle_emb = (summed / bundle_degree[:, None].astype(jnp.float32)).astype(jnp.bfloat16)
    mixed = jnp.dot(bundle_emb, weight, preferred_element_type=jnp.float32)
    activated = jax.nn.silu(mixed).astype(jnp.bfloat16)
    bundle_blocks = activated.reshape(-1, TILE, F)
    term2 = jnp.einsum(
        "tij,tjf->tif",
        tile2_values,
        bundle_blocks[tile2_source],
        preferred_element_type=jnp.float32,
    ).astype(jnp.bfloat16)
    where2 = placing(tile2_owner, width)
    buffer2, labels2 = bucketed(term2, tile2_slot, where2, width)
    got2, got_labels2 = (
        lax.all_to_all(buffer2, "wide", split_axis=0, concat_axis=0, tiled=True),
        lax.all_to_all(labels2, "wide", split_axis=0, concat_axis=0, tiled=True),
    )
    partial_value = collect(got2, got_labels2, group)
    degrees = user_degree[:, None].astype(jnp.float32)
    gathered = lax.psum(partial_value, "narrow")
    user_out = (gathered / degrees).astype(jnp.bfloat16)
    scaled_grad = (cotangent.astype(jnp.float32) / degrees).astype(jnp.bfloat16)
    grad_blocks = scaled_grad.reshape(-1, TILE, F)
    wanted = lax.all_to_all(labels2, "wide", split_axis=0, concat_axis=0, tiled=True)
    present = (wanted >= 0).astype(jnp.bfloat16)
    reply = grad_blocks[jnp.maximum(wanted, 0)] * present[:, :, None, None]
    back = lax.all_to_all(reply, "wide", split_axis=0, concat_axis=0, tiled=True)
    needed = back.reshape(width * CAP, TILE, F)[where2]
    term3 = jnp.einsum(
        "tji,tjf->tif", tile2_values, needed, preferred_element_type=jnp.float32
    ).astype(jnp.bfloat16)
    table = (tile2_source[None, :] == jnp.arange(bb_count, dtype=jnp.int32)[:, None]).astype(
        jnp.bfloat16
    )
    grad_act = jnp.dot(
        table, term3.reshape(-1, TILE * F), preferred_element_type=jnp.float32
    ).reshape(bb_count * TILE, F)
    sigma = jax.nn.sigmoid(mixed)
    grad_mixed = (grad_act * sigma * (1.0 + mixed * (1.0 - sigma))).astype(jnp.bfloat16)
    local_grad = lax.dot_general(
        bundle_emb, grad_mixed, (((0,), (0,)), ((), ())), preferred_element_type=jnp.float32
    )
    grad_weight = lax.psum(local_grad, ("wide", "narrow"))
    grad_bundle = lax.dot_general(
        grad_mixed, weight, (((1,), (1,)), ((), ())), preferred_element_type=jnp.float32
    ).astype(jnp.bfloat16)
    return (user_out, grad_weight, grad_bundle)


def solution(mesh):
    in_specs = (
        P(("wide", "narrow"), None),
        P(("wide", "narrow"), None, None),
        P(("wide", "narrow")),
        P(("wide", "narrow"), None),
        P(("wide", "narrow")),
        P(("wide", "narrow"), None, None),
        P(("wide", "narrow")),
        P(("wide", "narrow"), None),
        P(("wide", "narrow")),
        P(),
        P(("wide", "narrow")),
        P("wide"),
        P("wide", None),
    )
    out_specs = (P("wide", None), P(), P(("wide", "narrow"), None))
    return jax.shard_map(local, mesh=mesh, in_specs=in_specs, out_specs=out_specs, check_vma=False)
```

profile of v0, /device:TPU:0, one launch (start us, length us, event | category | flops | bytes accessed | tf_op | source)
XLA Modules:
  0.0 327.9 jit_solution(3484970495251447190)
XLA Ops:
  9.4 0.7 scatter_custom_fusion
  10.8 7.3 %all-to-all-start = ((s32[8,1,2]{2,1,0:T(1,128)}), s32[8,1,2]{2,1,0:T(1,128)S(1)}, u32[]{:S(2)}, u32[]{:S(2)}) async-start(s32[8,1,2]{2,1,0:T(1,128)} %bitcast.3), calls=%async_computation | async-start | bytes 8192 | tf_op jit(solution)/shard_map/all_to_all | solution.py:75
  21.7 1.5 gather_fusion
  23.2 1.4 fusion
  25.6 6.0 %all-to-all-start.1 = ((s32[8,1,2]{2,1,0:T(1,128)}), s32[8,1,2]{2,1,0:T(1,128)S(1)}, u32[]{:S(2)}, u32[]{:S(2)}) async-start(s32[8,1,2]{2,1,0:T(1,128)} %bitcast.7), calls=%async_computation.1 | async-start | bytes 8192 | tf_op jit(solution)/shard_map/all_to_all | solution.py:58
  31.6 1.1 broadcast.84.clone
  32.7 2.8 scatter_fusion
  35.5 2.5 all-to-all-done.1
  38.6 3.6 %all-to-all-start.2 = ((bf16[8,2,128,256]{3,2,1,0:T(8,128)(2,1)}), bf16[8,2,128,256]{3,2,1,0:T(8,128)(2,1)S(1)}, u32[]{:S(2)}, u32[]{:S(2)}) async-start(bf16[8,2,128,256]{3,2,1,0:T(8,128)(2,1)} %bitcast.10), calls=%async_computation.2 | async-start | bytes 2097152 | tf_op jit(solution)/shard_map/all_to_all | solution.py:57
  44.1 1.8 broadcast_multiply_fusion
  45.9 21.1 %all-to-all-done.2 = bf16[8,2,128,256]{3,2,1,0:T(8,128)(2,1)S(1)} async-done(((bf16[8,2,128,256]{3,2,1,0:T(8,128)(2,1)}), bf16[8,2,128,256]{3,2,1,0:T(8,128)(2,1)S(1)}, u32[]{:S(2)}, u32[]{:S(2)}) %all-to-all-start.2) | async-done | bytes 1048608 | tf_op jit(solution)/shard_map/all_to_all | solution.py:57
  67.0 3.6 %all-to-all-start.4 = ((bf16[8,2,128,256]{3,2,1,0:T(8,128)(2,1)}), bf16[8,2,128,256]{3,2,1,0:T(8,128)(2,1)S(1)}, u32[]{:S(2)}, u32[]{:S(2)}) async-start(bf16[8,2,128,256]{3,2,1,0:T(8,128)(2,1)} %broadcast_multiply_fusion), calls=%async_computation.4 | async-start | bytes 2097152 | tf_op jit(solution)/shard_map/all_to_all | solution.py:86
  73.3 23.1 %all-to-all-done.4 = bf16[8,2,128,256]{3,2,1,0:T(8,128)(2,1)S(1)} async-done(((bf16[8,2,128,256]{3,2,1,0:T(8,128)(2,1)}), bf16[8,2,128,256]{3,2,1,0:T(8,128)(2,1)S(1)}, u32[]{:S(2)}, u32[]{:S(2)}) %all-to-all-start.4) | async-done | bytes 1048608 | tf_op jit(solution)/shard_map/all_to_all | solution.py:86
  100.8 1.1 broadcast.84
  101.9 2.8 scatter_fusion.1
  104.7 3.6 %all-to-all-start.3 = ((bf16[8,2,128,256]{3,2,1,0:T(8,128)(2,1)}), bf16[8,2,128,256]{3,2,1,0:T(8,128)(2,1)S(1)}, u32[]{:S(2)}, u32[]{:S(2)}) async-start(bf16[8,2,128,256]{3,2,1,0:T(8,128)(2,1)} %bitcast.13), calls=%async_computation.3 | async-start | bytes 2097152 | tf_op jit(solution)/shard_map/all_to_all | solution.py:74
  109.1 25.2 %all-to-all-done.3 = bf16[8,2,128,256]{3,2,1,0:T(8,128)(2,1)S(1)} async-done(((bf16[8,2,128,256]{3,2,1,0:T(8,128)(2,1)}), bf16[8,2,128,256]{3,2,1,0:T(8,128)(2,1)S(1)}, u32[]{:S(2)}, u32[]{:S(2)}) %all-to-all-start.3) | async-done | bytes 1048608 | tf_op jit(solution)/shard_map/all_to_all | solution.py:74
  135.2 1.5 reshape.106
  136.8 1.0 convolution_convert_fusion.3
  137.8 1.0 fusion.18
  138.8 48.6 %all-reduce.3.cloned.1.call-done = f32[2048,256]{1,0:T(8,128)} async-done(((f32[2048,256]{1,0:T(8,128)}), f32[2048,256]{1,0:T(8,128)}) %all-reduce.3.cloned.1.call-update) | async-done | bytes 2097168 | tf_op jit(solution)/shard_map/psum | solution.py:79
  187.4 2.9 divide_convert_fusion.1
  190.3 129.1 %all-reduce.5.cloned.1.call-done = f32[256,256]{1,0:T(8,128)} async-done(((f32[256,256]{1,0:T(8,128)}), f32[256,256]{1,0:T(8,128)}) %all-reduce.5.cloned.1.call-update) | async-done | bytes 262160 | tf_op jit(solution)/shard_map/psum | solution.py:102
  319.4 1.7 copy.71
  (75 shorter events, 18.8 us)
Async XLA Ops:
  7.2 89.8 %copy-start = (bf16[12,128,128]{2,1,0:T(8,128)(2,1)S(1)}, bf16[12,128,128]{2,1,0:T(8,128)(2,1)}, u32[]{:S(2)}) copy-start(bf16[12,128,128]{2,1,0:T(8,128)(2,1)} %param.18) | copy-start | bytes 1179652
  9.4 9.4 %copy-start.6 = (s32[12]{0:T(128)}, s32[12]{0:T(128)S(1)}, u32[]{:S(2)}) copy-start(s32[12]{0:T(128)S(1)} %fusion.12) | copy-start | bytes 148
  10.8 14.8 %all-to-all-start = ((s32[8,1,2]{2,1,0:T(1,128)}), s32[8,1,2]{2,1,0:T(1,128)S(1)}, u32[]{:S(2)}, u32[]{:S(2)}) async-start(s32[8,1,2]{2,1,0:T(1,128)} %bitcast.3), calls=%async_computation | async-start | bytes 8192 | tf_op jit(solution)/shard_map/all_to_all | solution.py:75
  25.6 12.4 %all-to-all-start.1 = ((s32[8,1,2]{2,1,0:T(1,128)}), s32[8,1,2]{2,1,0:T(1,128)S(1)}, u32[]{:S(2)}, u32[]{:S(2)}) async-start(s32[8,1,2]{2,1,0:T(1,128)} %bitcast.7), calls=%async_computation.1 | async-start | bytes 8192 | tf_op jit(solution)/shard_map/all_to_all | solution.py:58
  32.7 9.5 %copy-start.5 = (s32[2048]{0:T(1024)S(1)}, s32[2048]{0:T(1024)}, u32[]{:S(2)}) copy-start(s32[2048]{0:T(1024)} %param.24) | copy-start | bytes 24580
  32.7 9.5 %copy-start.1 = (bf16[2048,256]{1,0:T(8,128)(2,1)S(1)}, bf16[2048,256]{1,0:T(8,128)(2,1)}, u32[]{:S(2)}) copy-start(bf16[2048,256]{1,0:T(8,128)(2,1)} %param.25) | copy-start | bytes 3145732
  38.0 0.6 copy-start.3
  38.6 28.4 %all-to-all-start.2 = ((bf16[8,2,128,256]{3,2,1,0:T(8,128)(2,1)}), bf16[8,2,128,256]{3,2,1,0:T(8,128)(2,1)S(1)}, u32[]{:S(2)}, u32[]{:S(2)}) async-start(bf16[8,2,128,256]{3,2,1,0:T(8,128)(2,1)} %bitcast.10), calls=%async_computation.2 | async-start | bytes 2097152 | tf_op jit(solution)/shard_map/all_to_all | solution.py:57
  44.1 27.0 %copy-start.4 = (s32[8,1,2]{2,1,0:T(1,128)S(1)}, s32[8,1,2]{2,1,0:T(1,128)}, u32[]{:S(2)}) copy-start(s32[8,1,2]{2,1,0:T(1,128)} %copy-done.3) | copy-start | bytes 196
  45.9 24.6 %copy-start.8 = (s32[512]{0:T(512)S(1)}, s32[512]{0:T(512)}, u32[]{:S(2)}) copy-start(s32[512]{0:T(512)} %param.23) | copy-start | bytes 6148
  45.9 24.6 %copy-start.7 = (s32[12]{0:T(128)S(1)}, s32[12]{0:T(128)}, u32[]{:S(2)}) copy-start(s32[12]{0:T(128)} %copy-done.6) | copy-start | bytes 148
  45.9 24.7 %copy-start.9 = (s32[12]{0:T(128)S(1)}, s32[12]{0:T(128)}, u32[]{:S(2)}) copy-start(s32[12]{0:T(128)} %param.19) | copy-start | bytes 148
  67.0 29.4 %all-to-all-start.4 = ((bf16[8,2,128,256]{3,2,1,0:T(8,128)(2,1)}), bf16[8,2,128,256]{3,2,1,0:T(8,128)(2,1)S(1)}, u32[]{:S(2)}, u32[]{:S(2)}) async-start(bf16[8,2,128,256]{3,2,1,0:T(8,128)(2,1)} %broadcast_multiply_fusion), calls=%async_computation.4 | async-start | bytes 2097152 | tf_op jit(solution)/shard_map/all_to_all | solution.py:86
  97.8 1.3 copy-start.2
  104.7 29.6 %all-to-all-start.3 = ((bf16[8,2,128,256]{3,2,1,0:T(8,128)(2,1)}), bf16[8,2,128,256]{3,2,1,0:T(8,128)(2,1)S(1)}, u32[]{:S(2)}, u32[]{:S(2)}) async-start(bf16[8,2,128,256]{3,2,1,0:T(8,128)(2,1)} %bitcast.13), calls=%async_computation.3 | async-start | bytes 2097152 | tf_op jit(solution)/shard_map/all_to_all | solution.py:74
  108.3 79.1 %all-reduce.3.cloned.1.call-start = ((), (), s32[]{:S(2)}) async-start(), calls=%async_computation.5 | async-start | bytes 4194304 | tf_op jit(solution)/shard_map/psum | solution.py:79
  136.7 182.7 %all-reduce.5.cloned.1.call-start = ((), (), s32[]{:S(2)}) async-start(), calls=%async_computation.6 | async-start | bytes 524288 | tf_op jit(solution)/shard_map/psum | solution.py:102
Sparse Core Ops, SparseCore 0:
  136.9 50.4 all-reduce.2
  194.3 125.0 all-reduce.4
where the time goes:
time: 329 us; the launch traced here: 328 us
  waiting for transfers between devices  250 us (76%)
  starting transfers between devices  24.1 us (7%)
  local copies, waits for them, and re-layouts  22.7 us (7%)
  between operations  14.4 us (4%)
  other arithmetic  11.6 us (4%)
  matrix products  5.58 us (2%)
    psum x1, waiting for transfers between devices, local(): grad_weight = lax.psum(local_grad, ('wide', 'narrow'))  129 us
    psum x1, waiting for transfers between devices, local(): gathered = lax.psum(partial_value, 'narrow')  48.6 us
    all_to_all x1, waiting for transfers between devices, local(): lax.all_to_all(buffer2, 'wide', split_axis=0, concat_axis=0, tiled=True)  25.2 us
    all_to_all x1, waiting for transfers between devices, local(): lax.all_to_all(reply, 'wide', split_axis=0, concat_axis=0, tiled=True)  23.1 us
    all_to_all x1, waiting for transfers between devices, local(): lax.all_to_all(buffer1, 'wide', split_axis=0, concat_axis=0, tiled=True)  21.1 us
    all_to_all x1, starting transfers between devices, local(): lax.all_to_all(labels2, 'wide', split_axis=0, concat_axis=0, tiled=True)  7.28 us
  transfers between devices with their start and end apart: 7, of which 6 were waited for; matrix products, arithmetic and copies ran while one was open for 7% of the time, Pallas kernels for 0%

commit v1 on v0

v1 whole, which is shorter than its diff:
```python
import functools

import jax
import jax.numpy as jnp
from jax import lax
from jax.experimental import pallas as pl
from jax.experimental.pallas import tpu as pltpu
from jax.sharding import PartitionSpec as P

F = 256
TILE = 128
CAP = 2
MESH = pl.DeviceIdType.MESH
f32 = jnp.float32
bf16 = jnp.bfloat16


def plan_kernel(width, tiles1, tiles2, owner1, slot1, owner2, slot2, table, count):
    size = width * CAP

    def clear(i, _):
        table[i] = 0
        table[size + i] = 0
        table[2 * size + i] = -1
        table[3 * size + i] = -1
        return 0

    lax.fori_loop(0, size, clear, 0)

    def reset(i, _):
        count[i] = 0
        return 0

    lax.fori_loop(0, 2 * width, reset, 0)

    def first(t, _):
        owner = owner1[t]
        place = owner * CAP + count[owner]
        count[owner] = count[owner] + 1
        table[place] = t
        table[2 * size + place] = slot1[t]
        return 0

    lax.fori_loop(0, tiles1, first, 0)

    def second(t, _):
        owner = owner2[t]
        place = owner * CAP + count[width + owner]
        count[width + owner] = count[width + owner] + 1
        table[size + place] = t
        table[3 * size + place] = slot2[t]
        table[4 * size + t] = place
        return 0

    lax.fori_loop(0, tiles2, second, 0)


def main_kernel(
    W, N, G, B, U, T2,
    table, source1, source2,
    items, tile1, tile2, weight, bdeg, udeg, cot,
    uout, gw_out, gb_out,
    labs, rlab, slab,
    send_a, send_c, recv_a, recv_b, recv_c,
    inv_u, scaled, acc1, emb, mixed, act, acc2, gact,
    gw_send, gw_recv, gw_part, gw_parts, gw_fin,
    red_send, red_recv,
    lab_s, lab_r, copy_sem, a_s, a_r, b_s, b_r, c_s, c_r,
    g1_s, g1_r, g2_s, g2_r, g3_s, g3_r, n_s, n_r,
):
    w = lax.axis_index("wide")
    n = lax.axis_index("narrow")
    H = W // G
    R = F // G
    SZ = W * CAP
    h, g = w // G, w % G

    def up(d):
        return lax.rem(w + d, W)

    def down(d):
        return lax.rem(w - d + W, W)

    def crossing(q):
        other = lax.rem(h * N + n + q, H * N)
        return (other // N) * G + g, other % N

    barrier = pltpu.get_barrier_semaphore()

    def greet(d, _):
        pl.semaphore_signal(barrier, inc=1, device_id=(up(d), n), device_id_type=MESH)
        return 0

    lax.fori_loop(1, W, greet, 0)

    def greet_cross(q, _):
        pl.semaphore_signal(barrier, inc=1, device_id=crossing(q), device_id_type=MESH)
        return 0

    lax.fori_loop(1, H * N, greet_cross, 0)
    if H > 1:
        def greet_group(d, _):
            peer = h * G + lax.rem(g + d, G)
            pl.semaphore_signal(barrier, inc=1, device_id=(peer, n), device_id_type=MESH)
            return 0

        lax.fori_loop(1, G, greet_group, 0)
    lane = lax.broadcasted_iota(jnp.int32, (8, 128), 1)

    def pack(o, _):
        v = jnp.zeros((8, 128), jnp.int32)
        for k in range(CAP):
            v = jnp.where(lane == k, table[2 * SZ + o * CAP + k], v)
            v = jnp.where(lane == CAP + k, table[3 * SZ + o * CAP + k], v)
        labs[o] = v
        return 0

    lax.fori_loop(0, W, pack, 0)
    rlab[w] = labs[w]
    pl.semaphore_wait(barrier, W - 1 + H * N - 1 + (G - 1 if H > 1 else 0))

    def remote(src, dst, ss, rs, dev):
        return pltpu.make_async_remote_copy(
            src_ref=src, dst_ref=dst, send_sem=ss, recv_sem=rs, device_id=dev, device_id_type=MESH
        )

    def wide_copy(src, dst, ss, rs, d):
        return remote(src.at[up(d)], dst.at[w], ss.at[d], rs.at[d], (up(d), n))

    def send_labels(d, _):
        wide_copy(labs, rlab, lab_s, lab_r, d).start()
        return 0

    lax.fori_loop(1, W, send_labels, 0)

    def term1(o, k):
        t = table[o * CAP + k]
        return jnp.dot(tile1[t], items[source1[t]], preferred_element_type=f32).astype(bf16)

    def send_terms1(d, _):
        o = up(d)
        for k in range(CAP):
            send_a[o, k] = term1(o, k)
        wide_copy(send_a, recv_a, a_s, a_r, d).start()
        return 0

    lax.fori_loop(1, W, send_terms1, 0)
    for k in range(CAP):
        recv_a[w, k] = term1(w, k)

    def scale(b, _):
        row = 1.0 / udeg[b].astype(f32)
        inv = jnp.transpose(jnp.broadcast_to(row, (TILE, TILE)))
        inv_u[b] = inv
        for c in range(F // TILE):
            cols = slice(c * TILE, (c + 1) * TILE)
            scaled[b, :, cols] = (cot[b, :, cols].astype(f32) * inv).astype(bf16)
        return 0

    lax.fori_loop(0, U, scale, 0)

    def wait_labels(d, _):
        c = wide_copy(labs, rlab, lab_s, lab_r, d)
        c.wait_send()
        c.wait_recv()
        return 0

    lax.fori_loop(1, W, wait_labels, 0)
    local = pltpu.make_async_copy(rlab, slab, copy_sem)
    local.start()
    local.wait()

    def wanted(o, k):
        return scaled[jnp.maximum(slab[o, 0, CAP + k], 0)]

    def send_replies(d, _):
        o = up(d)
        for k in range(CAP):
            send_c[o, k] = wanted(o, k)
        wide_copy(send_c, recv_c, c_s, c_r, d).start()
        return 0

    lax.fori_loop(1, W, send_replies, 0)
    for k in range(CAP):
        recv_c[w, k] = wanted(w, k)

    ROWS = 32

    def add_blocks(acc, recv, o, column, blocks):
        labels = [slab[o, 0, column + k] for k in range(CAP)]

        def part(r, _):
            rows = pl.ds(pl.multiple_of(r * ROWS, ROWS), ROWS)
            xs = [recv[o, k, rows, :].astype(f32) for k in range(CAP)]
            for b in range(blocks):
                total = acc[b, rows, :]
                for k in range(CAP):
                    total = total + xs[k] * (labels[k] == b).astype(f32)
                acc[b, rows, :] = total
            return 0

        lax.fori_loop(0, TILE // ROWS, part, 0)

    acc1[...] = jnp.zeros_like(acc1)
    add_blocks(acc1, recv_a, w, 0, B)

    def collect1(d, _):
        wide_copy(send_a, recv_a, a_s, a_r, d).wait_recv()
        add_blocks(acc1, recv_a, down(d), 0, B)
        return 0

    lax.fori_loop(1, W, collect1, 0)

    def transform(b, _):
        row = 1.0 / bdeg[b].astype(f32)
        inv = jnp.transpose(jnp.broadcast_to(row, (TILE, TILE)))
        for c in range(F // TILE):
            cols = slice(c * TILE, (c + 1) * TILE)
            emb[b, :, cols] = (acc1[b, :, cols] * inv).astype(bf16)
        m = jnp.dot(emb[b], weight[...], preferred_element_type=f32)
        mixed[b] = m
        act[b] = (m / (1.0 + jnp.exp(-m))).astype(bf16)
        return 0

    lax.fori_loop(0, B, transform, 0)

    def term2(o, k):
        t = table[SZ + o * CAP + k]
        return jnp.dot(tile2[t], act[source2[t]], preferred_element_type=f32).astype(bf16)

    def free_a(d, _):
        wide_copy(send_a, recv_a, a_s, a_r, d).wait_send()
        return 0

    lax.fori_loop(1, W, free_a, 0)

    def send_terms2(d, _):
        o = up(d)
        for k in range(CAP):
            send_a[o, k] = term2(o, k)
        wide_copy(send_a, recv_b, b_s, b_r, d).start()
        return 0

    lax.fori_loop(1, W, send_terms2, 0)
    for k in range(CAP):
        recv_b[w, k] = term2(w, k)

    def wait_replies(d, _):
        c = wide_copy(send_c, recv_c, c_s, c_r, d)
        c.wait_recv()
        c.wait_send()
        return 0

    acc2[...] = jnp.zeros_like(acc2)
    add_blocks(acc2, recv_b, w, CAP, U)
    gact[...] = jnp.zeros_like(gact)
    lax.fori_loop(1, W, wait_replies, 0)

    def back(t, _):
        place = table[4 * SZ + t]
        block = recv_c[place // CAP, place % CAP]
        x = lax.dot_general(
            tile2[t], block, (((0,), (0,)), ((), ())), preferred_element_type=f32
        )
        x = x.astype(bf16).astype(f32)
        for b in range(B):
            gact[b] += x * (source2[t] == b).astype(f32)
        return 0

    lax.fori_loop(0, T2, back, 0)

    def finish(b, total):
        m = mixed[b]
        s = 1.0 / (1.0 + jnp.exp(-m))
        gm = (gact[b] * s * (1.0 + m * (1.0 - s))).astype(bf16)
        gb_out[b] = lax.dot_general(
            gm, weight[...], (((1,), (1,)), ((), ())), preferred_element_type=f32
        ).astype(bf16)
        gw_out[...] += lax.dot_general(
            emb[b], gm, (((0,), (0,)), ((), ())), preferred_element_type=f32
        )
        return total

    gw_out[...] = jnp.zeros_like(gw_out)
    lax.fori_loop(0, B, finish, 0)

    for i in range(G):
        gw_send[i] = gw_out[i * R:(i + 1) * R, :].astype(bf16)

    def group(d):
        return lax.rem(g + d, G)

    def group_copy1(d):
        return remote(
            gw_send.at[group(d)], gw_recv.at[g], g1_s.at[d], g1_r.at[d], (h * G + group(d), n)
        )

    def cross_copy(q):
        return remote(gw_part, gw_parts.at[h * N + n], g2_s.at[q], g2_r.at[q], crossing(q))

    def group_copy3(d):
        return remote(
            gw_fin.at[g], gw_fin.at[g], g3_s.at[d], g3_r.at[d], (h * G + group(d), n)
        )

    def start_all(copy, size):
        def go(d, _):
            copy(d).start()
            return 0

        lax.fori_loop(1, size, go, 0)

    def wait_all(copy, size):
        def go(d, _):
            c = copy(d)
            c.wait_recv()
            c.wait_send()
            return 0

        lax.fori_loop(1, size, go, 0)

    start_all(group_copy1, G)
    gw_recv[g] = gw_send[g]

    def collect2(d, _):
        wide_copy(send_a, recv_b, b_s, b_r, d).wait_recv()
        add_blocks(acc2, recv_b, down(d), CAP, U)
        return 0

    half = W // 2
    lax.fori_loop(1, half, collect2, 0)
    wait_all(group_copy1, G)
    part = gw_recv[0].astype(f32)
    for i in range(1, G):
        part = part + gw_recv[i].astype(f32)
    gw_part[...] = part
    gw_parts[h * N + n] = part
    start_all(cross_copy, H * N)
    lax.fori_loop(half, W, collect2, 0)
    wait_all(cross_copy, H * N)
    part = gw_parts[0]
    for i in range(1, H * N):
        part = part + gw_parts[i]
    gw_fin[g] = part.astype(bf16)
    start_all(group_copy3, G)

    def free_b(d, _):
        wide_copy(send_a, recv_b, b_s, b_r, d).wait_send()
        return 0

    bits = N.bit_length() - 1
    size, base = U, 0
    spans = []
    for i in range(bits):
        size //= 2
        bit = (n // (1 << i)) % 2
        peer = n + (1 - 2 * bit) * (1 << i)
        mine, theirs = base + bit * size, base + (1 - bit) * size

        def ready(j, _, theirs=theirs):
            red_send[theirs + j] = acc2[theirs + j].astype(bf16)
            return 0

        lax.fori_loop(0, size, ready, 0)
        first = U - 2 * size
        c = remote(
            red_send.at[pl.ds(theirs, size)], red_recv.at[pl.ds(first, size)],
            n_s.at[i], n_r.at[i], (w, peer),
        )
        c.start()
        c.wait_recv()
        c.wait_send()

        def add(j, _, mine=mine, first=first):
            acc2[mine + j] += red_recv[first + j].astype(f32)
            return 0

        lax.fori_loop(0, size, add, 0)
        spans.append((mine, size, peer))
        base = mine

    def divide(j, _):
        b = base + j
        for c in range(F // TILE):
            cols = slice(c * TILE, (c + 1) * TILE)
            uout[b, :, cols] = (acc2[b, :, cols] * inv_u[b]).astype(bf16)
        return 0

    lax.fori_loop(0, size, divide, 0)
    for i, (mine, size, peer) in reversed(list(enumerate(spans))):
        span = uout.at[pl.ds(mine, size)]
        c = remote(span, span, n_s.at[bits + i], n_r.at[bits + i], (w, peer))
        c.start()
        c.wait_recv()
        c.wait_send()

    lax.fori_loop(1, W, free_b, 0)
    wait_all(group_copy3, G)
    for i in range(G):
        gw_out[i * R:(i + 1) * R, :] = gw_fin[i].astype(f32)


def local(
    items, tile1_values, tile1_source, tile1_owner, tile1_slot,
    tile2_values, tile2_source, tile2_owner, tile2_slot,
    weight, bundle_degree, user_degree, cotangent,
):
    W, N = lax.axis_size("wide"), lax.axis_size("narrow")
    G = min(W, 8)
    H = W // G
    B, U = bundle_degree.shape[0] // TILE, user_degree.shape[0] // TILE
    T1, T2 = tile1_values.shape[0], tile2_values.shape[0]
    R = F // G
    smem = pl.BlockSpec(memory_space=pltpu.SMEM)
    vmem = pl.BlockSpec(memory_space=pltpu.VMEM)
    table = pl.pallas_call(
        functools.partial(plan_kernel, W, T1, T2),
        out_shape=jax.ShapeDtypeStruct((4 * W * CAP + T2,), jnp.int32),
        in_specs=[smem] * 4,
        out_specs=smem,
        scratch_shapes=[pltpu.SMEM((2 * W,), jnp.int32)],
        name="plan",
    )(tile1_owner.reshape(-1), tile1_slot, tile2_owner.reshape(-1), tile2_slot)
    dma = pltpu.SemaphoreType.DMA
    bits = N.bit_length() - 1
    slots = (W, CAP, TILE, F)
    uout, gw, gb = pl.pallas_call(
        functools.partial(main_kernel, W, N, G, B, U, T2),
        out_shape=(
            jax.ShapeDtypeStruct((U, TILE, F), bf16),
            jax.ShapeDtypeStruct((F, F), f32),
            jax.ShapeDtypeStruct((B, TILE, F), bf16),
        ),
        in_specs=[smem] * 3 + [vmem] * 7,
        out_specs=(vmem,) * 3,
        scratch_shapes=[
            pltpu.VMEM((W, 8, 128), jnp.int32),
            pltpu.VMEM((W, 8, 128), jnp.int32),
            pltpu.SMEM((W, 8, 128), jnp.int32),
            pltpu.VMEM(slots, bf16),
            pltpu.VMEM(slots, bf16),
            pltpu.VMEM(slots, bf16),
            pltpu.VMEM(slots, bf16),
            pltpu.VMEM(slots, bf16),
            pltpu.VMEM((U, TILE, TILE), f32),
            pltpu.VMEM((U, TILE, F), bf16),
            pltpu.VMEM((B, TILE, F), f32),
            pltpu.VMEM((B, TILE, F), bf16),
            pltpu.VMEM((B, TILE, F), f32),
            pltpu.VMEM((B, TILE, F), bf16),
            pltpu.VMEM((U, TILE, F), f32),
            pltpu.VMEM((B, TILE, F), f32),
            pltpu.VMEM((G, R, F), bf16),
            pltpu.VMEM((G, R, F), bf16),
            pltpu.VMEM((R, F), f32),
            pltpu.VMEM((H * N, R, F), f32),
            pltpu.VMEM((G, R, F), bf16),
            pltpu.VMEM((U, TILE, F), bf16),
            pltpu.VMEM((U, TILE, F), bf16),
            dma((W,)), dma((W,)), dma,
            dma((W,)), dma((W,)), dma((W,)), dma((W,)), dma((W,)), dma((W,)),
            dma((G,)), dma((G,)), dma((H * N,)), dma((H * N,)), dma((G,)), dma((G,)),
            dma((2 * bits,)), dma((2 * bits,)),
        ],
        compiler_params=pltpu.CompilerParams(
            collective_id=0, has_side_effects=True, vmem_limit_bytes=60 * 1024 * 1024
        ),
        name="hypergraph",
    )(
        table, tile1_source, tile2_source,
        items.reshape(-1, TILE, F), tile1_values, tile2_values, weight,
        bundle_degree.reshape(B, 1, TILE), user_degree.reshape(U, 1, TILE),
        cotangent.reshape(U, TILE, F),
    )
    return uout.reshape(U * TILE, F), gw, gb.reshape(B * TILE, F)


def solution(mesh):
    both = ("wide", "narrow")
    in_specs = (
        P(both, None), P(both, None, None), P(both), P(both, None), P(both),
        P(both, None, None), P(both), P(both, None), P(both),
        P(), P(both), P("wide"), P("wide", None),
    )
    out_specs = (P("wide", None), P(), P(both, None))
    return jax.shard_map(local, mesh=mesh, in_specs=in_specs, out_specs=out_specs, check_vma=False)
```

time: 329 us -> 111 us (0.34)
  waiting for transfers between devices: 250 us -> 0 us
  Pallas kernels: 0 us -> 106 us
  starting transfers between devices: 24.1 us -> 0 us
  local copies, waits for them, and re-layouts: 22.7 us -> 4.05 us
  between operations: 14.4 us -> 0.66 us
  other arithmetic: 11.6 us -> 0 us
  matrix products: 5.58 us -> 0 us
    psum x2 -> x0, waiting for transfers between devices: 178 us -> none  [the longest x1 129 us: local(): grad_weight = lax.psum(local_grad, ('wide', 'narrow'))]
    pallas_call x0 -> x2, Pallas kernels: none -> 106 us  [the longest x1 104 us: local(): pl.pallas_call(functools.partial(main_kernel, W, N, G, B, U, T2), out_sha...]
    all_to_all x5 -> x0, waiting for transfers between devices: 71.8 us -> none  [the longest x1 25.2 us: local(): lax.all_to_all(buffer2, 'wide', split_axis=0, concat_axis=0, tiled=True)]
    all_to_all x5 -> x0, starting transfers between devices: 24 us -> none  [the longest x1 7.28 us: local(): lax.all_to_all(labels2, 'wide', split_axis=0, concat_axis=0, tiled=True)]
    scatter x4 -> x0, local copies, waits for them, and re-layouts: 7.06 us -> none  [the longest x2 5.58 us: bucketed(): jnp.zeros((width * CAP, TILE, F), jnp.bfloat16).at[where].set(terms)]
    dot_general x9 -> x0, matrix products: 5.58 us -> none  [the longest x1 1.42 us: local(): jnp.einsum('tij,tjf->tif', tile1_values, item_blocks[tile1_source], prefe...]
    convert_element_type x8 -> x0, other arithmetic: 4.77 us -> none  [the longest x1 2.9 us: local(): user_out = (gathered / degrees).astype(jnp.bfloat16)]
    gather x4 -> x0, local copies, waits for them, and re-layouts: 3.36 us -> none  [the longest x1 1.55 us: local(): item_blocks[tile1_source]]
  transfers between devices with their start and end apart: 7 -> 0, of which waited for: 6 -> 0; matrix products, arithmetic and copies ran while one was open for 7% -> 0% of each run, Pallas kernels for 0% -> 0%
where the time goes in v1:
time: 111 us; the launch traced here: 110 us
  Pallas kernels  106 us (95%)
  local copies, waits for them, and re-layouts  4.05 us (4%)
    pallas_call x1, Pallas kernels, local(): pl.pallas_call(functools.partial(main_kernel, W, N, G, B, U, T2), out_sha...  104 us
    unnamed x7, local copies, waits for them, and re-layouts  4.05 us

profile of v1, /device:TPU:0, one launch (start us, length us, event | category | flops | bytes accessed | tf_op | source)
XLA Modules:
  0.0 110.3 jit_solution(14944091290910695735)
XLA Ops:
  0.6 1.8 %plan.1.table = s32[76]{0:T(128)} custom-call(s32[12]{0:T(128)} %bitcast.14, s32[12]{0:T(128)} %slot1.1, s32[12]{0:T(128)} %bitcast.15, s32[12]{0:T(128)} %slot2.1), custom_call_target="tpu_custom_call" | custom-call | tf_op jit(solution)/shard_map/plan/pallas_call | solution.py:416
  2.4 103.9 %hypergraph.1 = (bf16[16,128,256]{2,1,0:T(8,128)(2,1)}, f32[256,256]{1,0:T(8,128)}, bf16[4,128,256]{2,1,0:T(8,128)(2,1)}) custom-call(s32[76]{0:T(128)} %plan.1.table, s32[12]{0:T(128)} %source1.1, s32[12]{0:T(128)} %source2.1, bf16[4,128,256]{2,1,0:T(8,128)(2,1)} %bitcast.11, bf16[12,128,128]{2,1,0:T(8,128)(2,1)} %tile1.1, bf16[12,128,128]{2,1,0:T(8,128)(2,1)} %tile2.1, ...), custom_call_target="tpu_custom_call" | custom-call | tf_op jit(solution)/shard_map/hypergraph/pallas_call | solution.py:427
  106.3 0.0 copy-start.1
  106.3 2.3 %copy.19 = bf16[2048,256]{1,0:T(8,128)(2,1)} copy(bf16[2048,256]{1,0:T(8,128)(2,1)} %bitcast.8) | data formatting | bytes 2097152
  108.6 0.0 copy-done.1
  108.6 0.0 copy-start
  108.6 0.7 copy.20
  109.3 0.3 copy-done
  109.6 0.7 copy.21
Async XLA Ops:
  106.3 2.3 %copy-start.1 = (f32[256,256]{1,0:T(8,128)S(1)}, f32[256,256]{1,0:T(8,128)}, u32[]{:S(2)}) copy-start(f32[256,256]{1,0:T(8,128)} %get-tuple-element.13) | copy-start | bytes 786436
  108.6 1.0 copy-start

commit v2 on v1

--- a/solution.py
+++ b/solution.py
@@ -62,11 +62,11 @@
     uout, gw_out, gb_out,
     labs, rlab, slab,
     send_a, send_c, recv_a, recv_b, recv_c,
-    inv_u, scaled, acc1, emb, mixed, act, acc2, gact,
+    inv_u, scaled, relay, half_send, half_recv, acc1, gact, emb, mixed, act, acc2,
     gw_send, gw_recv, gw_part, gw_parts, gw_fin,
     red_send, red_recv,
     lab_s, lab_r, copy_sem, a_s, a_r, b_s, b_r, c_s, c_r,
-    g1_s, g1_r, g2_s, g2_r, g3_s, g3_r, n_s, n_r,
+    g1_s, g1_r, g2_s, g2_r, g3_s, g3_r, n_s, n_r, r_s, r_r, h_s, h_r,
 ):
     w = lax.axis_index("wide")
     n = lax.axis_index("narrow")
@@ -74,6 +74,11 @@
     R = F // G
     SZ = W * CAP
     h, g = w // G, w % G
+    Q = W // 2
+    side, place_in = w // Q, w % Q
+    pair = lax.rem(w + Q, W)
+    C = F // TILE
+    bits = N.bit_length() - 1
 
     def up(d):
         return lax.rem(w + d, W)
@@ -112,6 +117,9 @@
         for k in range(CAP):
             v = jnp.where(lane == k, table[2 * SZ + o * CAP + k], v)
             v = jnp.where(lane == CAP + k, table[3 * SZ + o * CAP + k], v)
+            far = lax.rem(o + Q, W) * CAP + k
+            v = jnp.where(lane == 2 * CAP + k, table[2 * SZ + far], v)
+            v = jnp.where(lane == 3 * CAP + k, table[3 * SZ + far], v)
         labs[o] = v
         return 0
 
@@ -133,31 +141,76 @@
 
     lax.fori_loop(1, W, send_labels, 0)
 
+    spans = []
+    size, base = U, 0
+    for i in range(bits):
+        size //= 2
+        bit = (n // (1 << i)) % 2
+        peer = n + (1 - 2 * bit) * (1 << i)
+        spans.append((base + bit * size, base + (1 - bit) * size, size, peer))
+        base = base + bit * size
+
+    def scale(b):
+        row = 1.0 / udeg[b].astype(f32)
+        inv = jnp.transpose(jnp.broadcast_to(row, (TILE, TILE)))
+        inv_u[b] = inv
+        for c in range(C):
+            cols = slice(c * TILE, (c + 1) * TILE)
+            scaled[b, :, cols] = (cot[b, :, cols].astype(f32) * inv).astype(bf16)
+
+    def scale_first(j, _):
+        scale(base + j)
+        return 0
+
+    def scale_rest(j, _):
+        scale(lax.rem(base + j, U))
+        return 0
+
+    lax.fori_loop(0, size, scale_first, 0)
+    over = remote(
+        scaled.at[pl.ds(base, size)], relay.at[pl.ds(base, size)], h_s.at[0], h_r.at[0], (pair, n)
+    )
+    over.start()
+
+    def mate(d):
+        return side * Q + lax.rem(place_in + d, Q)
+
+    def mate_back(d):
+        return side * Q + lax.rem(place_in - d + Q, Q)
+
+    def far(o):
+        return lax.rem(o + Q, W)
+
+    def near_copy(src, dst, ss, rs, d):
+        return remote(src.at[mate(d)], dst.at[w], ss.at[d], rs.at[d], (mate(d), n))
+
+    def far_copy(src, dst, ss, rs, d):
+        return remote(src.at[far(mate(d))], dst.at[pair], ss.at[Q + d], rs.at[Q + d], (mate(d), n))
+
     def term1(o, k):
         t = table[o * CAP + k]
         return jnp.dot(tile1[t], items[source1[t]], preferred_element_type=f32).astype(bf16)
 
-    def send_terms1(d, _):
-        o = up(d)
+    def send_far1(d, _):
+        o = far(mate(d))
         for k in range(CAP):
             send_a[o, k] = term1(o, k)
-        wide_copy(send_a, recv_a, a_s, a_r, d).start()
-        return 0
-
-    lax.fori_loop(1, W, send_terms1, 0)
+        far_copy(send_a, recv_a, a_s, a_r, d).start()
+        return 0
+
+    def send_near1(d, _):
+        o = mate(d)
+        for k in range(CAP):
+            send_a[o, k] = term1(o, k)
+        near_copy(send_a, recv_a, a_s, a_r, d).start()
+        return 0
+
+    lax.fori_loop(1, Q, send_far1, 0)
+    lax.fori_loop(1, Q, send_near1, 0)
     for k in range(CAP):
+        recv_a[pair, k] = term1(pair, k)
         recv_a[w, k] = term1(w, k)
-
-    def scale(b, _):
-        row = 1.0 / udeg[b].astype(f32)
-        inv = jnp.transpose(jnp.broadcast_to(row, (TILE, TILE)))
-        inv_u[b] = inv
-        for c in range(F // TILE):
-            cols = slice(c * TILE, (c + 1) * TILE)
-            scaled[b, :, cols] = (cot[b, :, cols].astype(f32) * inv).astype(bf16)
-        return 0
-
-    lax.fori_loop(0, U, scale, 0)
+    lax.fori_loop(size, U, scale_rest, 0)
 
     def wait_labels(d, _):
         c = wide_copy(labs, rlab, lab_s, lab_r, d)
@@ -170,46 +223,90 @@
     local.start()
     local.wait()
 
-    def wanted(o, k):
-        return scaled[jnp.maximum(slab[o, 0, CAP + k], 0)]
-
-    def send_replies(d, _):
-        o = up(d)
-        for k in range(CAP):
-            send_c[o, k] = wanted(o, k)
-        wide_copy(send_c, recv_c, c_s, c_r, d).start()
-        return 0
-
-    lax.fori_loop(1, W, send_replies, 0)
-    for k in range(CAP):
-        recv_c[w, k] = wanted(w, k)
-
     ROWS = 32
 
-    def add_blocks(acc, recv, o, column, blocks):
+    def add_blocks(acc, recv, place, o, column, blocks, cols):
         labels = [slab[o, 0, column + k] for k in range(CAP)]
 
         def part(r, _):
             rows = pl.ds(pl.multiple_of(r * ROWS, ROWS), ROWS)
-            xs = [recv[o, k, rows, :].astype(f32) for k in range(CAP)]
+            xs = [recv[place, k, rows, cols].astype(f32) for k in range(CAP)]
             for b in range(blocks):
-                total = acc[b, rows, :]
+                total = acc[b, rows, cols]
                 for k in range(CAP):
                     total = total + xs[k] * (labels[k] == b).astype(f32)
-                acc[b, rows, :] = total
+                acc[b, rows, cols] = total
             return 0
 
         lax.fori_loop(0, TILE // ROWS, part, 0)
 
+    every = slice(0, F)
+    gact[...] = jnp.zeros_like(gact)
+    add_blocks(gact, recv_a, pair, w, 2 * CAP, B, every)
+
+    def collect_far(d, _):
+        far_copy(send_a, recv_a, a_s, a_r, d).wait_recv()
+        o = mate_back(d)
+        add_blocks(gact, recv_a, far(o), o, 2 * CAP, B, every)
+        return 0
+
+    lax.fori_loop(1, Q, collect_far, 0)
+    half_send[...] = gact[...].astype(bf16)
+    across = remote(half_send, half_recv, h_s.at[1], h_r.at[1], (pair, n))
+    across.start()
+
+    def near_block(o, k):
+        return scaled[jnp.maximum(slab[o, 0, CAP + k], 0)]
+
+    def far_block(o, k):
+        return relay[jnp.maximum(slab[o, 0, 3 * CAP + k], 0)]
+
+    def send_near_replies(d, _):
+        o = mate(d)
+        for k in range(CAP):
+            send_c[o, k] = near_block(o, k)
+        near_copy(send_c, recv_c, c_s, c_r, d).start()
+        return 0
+
+    def send_far_replies(d, _):
+        o = mate(d)
+        for k in range(CAP):
+            send_c[far(o), k] = far_block(o, k)
+        far_copy(send_c, recv_c, c_s, c_r, d).start()
+        return 0
+
+    def relay_copy(i):
+        mine, _, many, peer = spans[i]
+        span = relay.at[pl.ds(mine, many)]
+        return remote(span, span, r_s.at[i], r_r.at[i], (w, peer))
+
+    over.wait_recv()
+    relay_copy(bits - 1).start()
+    lax.fori_loop(1, Q, send_near_replies, 0)
+    for k in range(CAP):
+        recv_c[w, k] = near_block(w, k)
+
     acc1[...] = jnp.zeros_like(acc1)
-    add_blocks(acc1, recv_a, w, 0, B)
-
-    def collect1(d, _):
-        wide_copy(send_a, recv_a, a_s, a_r, d).wait_recv()
-        add_blocks(acc1, recv_a, down(d), 0, B)
-        return 0
-
-    lax.fori_loop(1, W, collect1, 0)
+    add_blocks(acc1, recv_a, w, w, 0, B, every)
+
+    def collect_near(d, _):
+        near_copy(send_a, recv_a, a_s, a_r, d).wait_recv()
+        o = mate_back(d)
+        add_blocks(acc1, recv_a, o, o, 0, B, every)
+        return 0
+
+    for i in range(bits - 1, -1, -1):
+        relay_copy(i).wait_recv()
+        relay_copy(i).wait_send()
+        if i > 0:
+            relay_copy(i - 1).start()
+        if i == bits - 1:
+            lax.fori_loop(1, Q, collect_near, 0)
+    lax.fori_loop(1, Q, send_far_replies, 0)
+    for k in range(CAP):
+        recv_c[pair, k] = far_block(w, k)
+    across.wait_recv()
+    acc1[...] += half_recv[...].astype(f32)
 
     def transform(b, _):
         row = 1.0 / bdeg[b].astype(f32)
@@ -229,16 +326,26 @@
         return jnp.dot(tile2[t], act[source2[t]], preferred_element_type=f32).astype(bf16)
 
     def free_a(d, _):
-        wide_copy(send_a, recv_a, a_s, a_r, d).wait_send()
-        return 0
-
-    lax.fori_loop(1, W, free_a, 0)
+        near_copy(send_a, recv_a, a_s, a_r, d).wait_send()
+        far_copy(send_a, recv_a, a_s, a_r, d).wait_send()
+        return 0
+
+    lax.fori_loop(1, Q, free_a, 0)
+
+    def column(c):
+        return slice(c * TILE, (c + 1) * TILE)
+
+    def user_copy(c, d):
+        return remote(
+            send_a.at[up(d), :, :, column(c)], recv_b.at[w, :, :, column(c)],
+            b_s.at[c, d], b_r.at[c, d], (up(d), n),
+        )
 
     def send_terms2(d, _):
         o = up(d)
         for k in range(CAP):
             send_a[o, k] = term2(o, k)
-        wide_copy(send_a, recv_b, b_s, b_r, d).start()
+        user_copy(0, d).start()
         return 0
 
     lax.fori_loop(1, W, send_terms2, 0)
@@ -246,15 +353,15 @@
         recv_b[w, k] = term2(w, k)
 
     def wait_replies(d, _):
-        c = wide_copy(send_c, recv_c, c_s, c_r, d)
-        c.wait_recv()
-        c.wait_send()
+        for c in (near_copy(send_c, recv_c, c_s, c_r, d), far_copy(send_c, recv_c, c_s, c_r, d)):
+            c.wait_recv()
+            c.wait_send()
         return 0
 
     acc2[...] = jnp.zeros_like(acc2)
-    add_blocks(acc2, recv_b, w, CAP, U)
+    add_blocks(acc2, recv_b, w, w, CAP, U, every)
     gact[...] = jnp.zeros_like(gact)
-    lax.fori_loop(1, W, wait_replies, 0)
+    lax.fori_loop(1, Q, wait_replies, 0)
 
     def back(t, _):
         place = table[4 * SZ + t]
@@ -268,6 +375,14 @@
         return 0
 
     lax.fori_loop(0, T2, back, 0)
+
+    def send_later(d, _):
+        user_copy(0, d).wait_send()
+        for c in range(1, C):
+            user_copy(c, d).start()
+        return 0
+
+    lax.fori_loop(1, W, send_later, 0)
 
     def finish(b, total):
         m = mixed[b]
@@ -322,13 +437,79 @@
     start_all(group_copy1, G)
     gw_recv[g] = gw_send[g]
 
-    def collect2(d, _):
-        wide_copy(send_a, recv_b, b_s, b_r, d).wait_recv()
-        add_blocks(acc2, recv_b, down(d), CAP, U)
-        return 0
-
-    half = W // 2
-    lax.fori_loop(1, half, collect2, 0)
+    def collect2(c):
+        def go(d, _):
+            user_copy(c, d).wait_recv()
+            add_blocks(acc2, recv_b, down(d), down(d), CAP, U, column(c))
+            return 0
+
+        return go
+
+    def halve_copy(c, i):
+        _, theirs, many, peer = spans[i]
+        return remote(
+            red_send.at[c, pl.ds(theirs, many)], red_recv.at[c, pl.ds(U - 2 * many, many)],
+            n_s.at[c, i], n_r.at[c, i], (w, peer),
+        )
+
+    def double_copy(c, i):
+        mine, _, many, peer = spans[i]
+        span = uout.at[pl.ds(mine, many), :, column(c)]
+        return remote(span, span, n_s.at[c, bits + i], n_r.at[c, bits + i], (w, peer))
+
+    def halve_start(c, i):
+        _, theirs, many, _ = spans[i]
+
+        def ready(j, _):
+            red_send[c, theirs + j] = acc2[theirs + j, :, column(c)].astype(bf16)
+            return 0
+
+        lax.fori_loop(0, many, ready, 0)
+        halve_copy(c, i).start()
+
+    def halve_end(c, i):
+        mine, _, many, _ = spans[i]
+        x = halve_copy(c, i)
+        x.wait_recv()
+        x.wait_send()
+
+        def add(j, _):
+            acc2[mine + j, :, column(c)] += red_recv[c, U - 2 * many + j].astype(f32)
+            return 0
+
+        lax.fori_loop(0, many, add, 0)
+
+    def divide(c):
+        def go(j, _):
+            b = base + j
+            uout[b, :, column(c)] = (acc2[b, :, column(c)] * inv_u[b]).astype(bf16)
+            return 0
+
+        lax.fori_loop(0, size, go, 0)
+
+    def double_end(c, i):
+        x = double_copy(c, i)
+        x.wait_recv()
+        x.wait_send()
+
+    def narrow_step(c, step):
+        if step < bits:
+            if step > 0:
+                halve_end(c, step - 1)
+            halve_start(c, step)
+        elif step < 2 * bits:
+            i = 2 * bits - 1 - step
+            if step == bits:
+                halve_end(c, bits - 1)
+                divide(c)
+            else:
+                double_end(c, i + 1)
+            double_copy(c, i).start()
+        else:
+            double_end(c, 0)
+
+    lax.fori_loop(1, W, collect2(0), 0)
+    narrow_step(0, 0)
     wait_all(group_copy1, G)
     part = gw_recv[0].astype(f32)
     for i in range(1, G):
@@ -336,64 +517,31 @@
     gw_part[...] = part
     gw_parts[h * N + n] = part
     start_all(cross_copy, H * N)
-    lax.fori_loop(half, W, collect2, 0)
-    wait_all(cross_copy, H * N)
-    part = gw_parts[0]
-    for i in range(1, H * N):
-        part = part + gw_parts[i]
-    gw_fin[g] = part.astype(bf16)
-    start_all(group_copy3, G)
+    steps = 2 * bits
+    for c in range(1, C):
+        for step in range(1, steps + 1):
+            narrow_step(c - 1, step)
+            if step == 1 and c == 1:
+                wait_all(cross_copy, H * N)
+                part = gw_parts[0]
+                for i in range(1, H * N):
+                    part = part + gw_parts[i]
+                gw_fin[g] = part.astype(bf16)
+                start_all(group_copy3, G)
+            lo = 1 + (W - 1) * (step - 1) // steps
+            hi = 1 + (W - 1) * step // steps
+            lax.fori_loop(lo, hi, collect2(c), 0)
+        narrow_step(c, 0)
+    for step in range(1, steps + 1):
+        narrow_step(C - 1, step)
 
     def free_b(d, _):
-        wide_copy(send_a, recv_b, b_s, b_r, d).wait_send()
-        return 0
-
-    bits = N.bit_length() - 1
-    size, base = U, 0
-    spans = []
-    for i in range(bits):
-        size //= 2
-        bit = (n // (1 << i)) % 2
-        peer = n + (1 - 2 * bit) * (1 << i)
-        mine, theirs = base + bit * size, base + (1 - bit) * size
-
-        def ready(j, _, theirs=theirs):
-            red_send[theirs + j] = acc2[theirs + j].astype(bf16)
-            return 0
-
-        lax.fori_loop(0, size, ready, 0)
-        first = U - 2 * size
-        c = remote(
-            red_send.at[pl.ds(theirs, size)], red_recv.at[pl.ds(first, size)],
-            n_s.at[i], n_r.at[i], (w, peer),
-        )
-        c.start()
-        c.wait_recv()
-        c.wait_send()
-
-        def add(j, _, mine=mine, first=first):
-            acc2[mine + j] += red_recv[first + j].astype(f32)
-            return 0
-
-        lax.fori_loop(0, size, add, 0)
-        spans.append((mine, size, peer))
-        base = mine
-
-    def divide(j, _):
-        b = base + j
-        for c in range(F // TILE):
-            cols = slice(c * TILE, (c + 1) * TILE)
-            uout[b, :, cols] = (acc2[b, :, cols] * inv_u[b]).astype(bf16)
-        return 0
-
-    lax.fori_loop(0, size, divide, 0)
-    for i, (mine, size, peer) in reversed(list(enumerate(spans))):
-        span = uout.at[pl.ds(mine, size)]
-        c = remote(span, span, n_s.at[bits + i], n_r.at[bits + i], (w, peer))
-        c.start()
-        c.wait_recv()
-        c.wait_send()
-
+        for c in range(1, C):
+            user_copy(c, d).wait_send()
+        return 0
+
+    over.wait_send()
+    across.wait_send()
     lax.fori_loop(1, W, free_b, 0)
     wait_all(group_copy3, G)
     for i in range(G):
@@ -444,26 +592,30 @@
             pltpu.VMEM(slots, bf16),
             pltpu.VMEM((U, TILE, TILE), f32),
             pltpu.VMEM((U, TILE, F), bf16),
+            pltpu.VMEM((U, TILE, F), bf16),
+            pltpu.VMEM((B, TILE, F), bf16),
+            pltpu.VMEM((B, TILE, F), bf16),
+            pltpu.VMEM((B, TILE, F), f32),
             pltpu.VMEM((B, TILE, F), f32),
             pltpu.VMEM((B, TILE, F), bf16),
             pltpu.VMEM((B, TILE, F), f32),
             pltpu.VMEM((B, TILE, F), bf16),
             pltpu.VMEM((U, TILE, F), f32),
-            pltpu.VMEM((B, TILE, F), f32),
             pltpu.VMEM((G, R, F), bf16),
             pltpu.VMEM((G, R, F), bf16),
             pltpu.VMEM((R, F), f32),
             pltpu.VMEM((H * N, R, F), f32),
             pltpu.VMEM((G, R, F), bf16),
-            pltpu.VMEM((U, TILE, F), bf16),
-            pltpu.VMEM((U, TILE, F), bf16),
+            pltpu.VMEM((F // TILE, U, TILE, TILE), bf16),
+            pltpu.VMEM((F // TILE, U, TILE, TILE), bf16),
             dma((W,)), dma((W,)), dma,
-            dma((W,)), dma((W,)), dma((W,)), dma((W,)), dma((W,)), dma((W,)),
+            dma((W,)), dma((W,)), dma((F // TILE, W)), dma((F // TILE, W)), dma((W,)), dma((W,)),
             dma((G,)), dma((G,)), dma((H * N,)), dma((H * N,)), dma((G,)), dma((G,)),
-            dma((2 * bits,)), dma((2 * bits,)),
+            dma((F // TILE, 2 * bits)), dma((F // TILE, 2 * bits)), dma((bits,)), dma((bits,)),
+            dma((2,)), dma((2,)),
         ],
         compiler_params=pltpu.CompilerParams(
-            collective_id=0, has_side_effects=True, vmem_limit_bytes=60 * 1024 * 1024
+            collective_id=0, has_side_effects=True, vmem_limit_bytes=61 * 1024 * 1024
         ),
         name="hypergraph",
     )(

time: 111 us -> 96.6 us (0.87)
  Pallas kernels: 106 us -> 90.9 us
    pallas_call x1, Pallas kernels: 104 us -> 89.1 us  [local(): pl.pallas_call(functools.partial(main_kernel, W, N, G, B, U, T2), out_sha...]
where the time goes in v2:
time: 96.6 us; the launch traced here: 95.6 us
  Pallas kernels  90.9 us (94%)
  local copies, waits for them, and re-layouts  4.05 us (4%)
    pallas_call x1, Pallas kernels, local(): pl.pallas_call(functools.partial(main_kernel, W, N, G, B, U, T2), out_sha...  89.1 us
    unnamed x7, local copies, waits for them, and re-layouts  4.05 us

profile of v2, /device:TPU:0, one launch (start us, length us, event | category | flops | bytes accessed | tf_op | source)
XLA Modules:
  0.0 95.6 jit_solution(4458812132198959704)
XLA Ops:
  0.6 1.8 %plan.1.table = s32[76]{0:T(128)} custom-call(s32[12]{0:T(128)} %bitcast.14, s32[12]{0:T(128)} %slot1.1, s32[12]{0:T(128)} %bitcast.15, s32[12]{0:T(128)} %slot2.1), custom_call_target="tpu_custom_call" | custom-call | tf_op jit(solution)/shard_map/plan/pallas_call | solution.py:564
  2.4 89.1 %hypergraph.1 = (bf16[16,128,256]{2,1,0:T(8,128)(2,1)}, f32[256,256]{1,0:T(8,128)}, bf16[4,128,256]{2,1,0:T(8,128)(2,1)}) custom-call(s32[76]{0:T(128)} %plan.1.table, s32[12]{0:T(128)} %source1.1, s32[12]{0:T(128)} %source2.1, bf16[4,128,256]{2,1,0:T(8,128)(2,1)} %bitcast.11, bf16[12,128,128]{2,1,0:T(8,128)(2,1)} %tile1.1, bf16[12,128,128]{2,1,0:T(8,128)(2,1)} %tile2.1, ...), custom_call_target="tpu_custom_call" | custom-call | tf_op jit(solution)/shard_map/hypergraph/pallas_call | solution.py:575
  91.5 0.0 copy-start.1
  91.5 2.3 %copy.19 = bf16[2048,256]{1,0:T(8,128)(2,1)} copy(bf16[2048,256]{1,0:T(8,128)(2,1)} %bitcast.8) | data formatting | bytes 2097152
  93.8 0.0 copy-done.1
  93.8 0.0 copy-start
  93.8 0.7 copy.20
  94.5 0.3 copy-done
  94.9 0.7 copy.21
Async XLA Ops:
  91.5 2.3 %copy-start.1 = (f32[256,256]{1,0:T(8,128)S(1)}, f32[256,256]{1,0:T(8,128)}, u32[]{:S(2)}) copy-start(f32[256,256]{1,0:T(8,128)} %get-tuple-element.13) | copy-start | bytes 786436
  93.8 1.0 %copy-start = (bf16[4,128,256]{2,1,0:T(8,128)(2,1)S(1)}, bf16[4,128,256]{2,1,0:T(8,128)(2,1)}, u32[]{:S(2)}) copy-start(bf16[4,128,256]{2,1,0:T(8,128)(2,1)} %get-tuple-element.8) | copy-start | bytes 786436

commit v3 on v2

--- a/solution.py
+++ b/solution.py
@@ -198,20 +198,26 @@
         far_copy(send_a, recv_a, a_s, a_r, d).start()
         return 0
 
-    def send_near1(d, _):
+    def make_near1(d, _):
         o = mate(d)
         for k in range(CAP):
             send_a[o, k] = term1(o, k)
-        near_copy(send_a, recv_a, a_s, a_r, d).start()
         return 0
 
     lax.fori_loop(1, Q, send_far1, 0)
-    lax.fori_loop(1, Q, send_near1, 0)
+    lax.fori_loop(1, Q, make_near1, 0)
     for k in range(CAP):
         recv_a[pair, k] = term1(pair, k)
         recv_a[w, k] = term1(w, k)
     lax.fori_loop(size, U, scale_rest, 0)
 
+    def release_near1(d, _):
+        far_copy(send_a, recv_a, a_s, a_r, d).wait_send()
+        near_copy(send_a, recv_a, a_s, a_r, d).start()
+        return 0
+
+    lax.fori_loop(1, Q, release_near1, 0)
+
     def wait_labels(d, _):
         c = wide_copy(labs, rlab, lab_s, lab_r, d)
         c.wait_send()
@@ -219,7 +225,7 @@
         return 0
 
     lax.fori_loop(1, W, wait_labels, 0)
-    local = pltpu.make_async_copy(rlab, slab, copy_sem)
+    local = pltpu.make_async_copy(rlab.at[:, pl.ds(0, 1), :], slab, copy_sem)
     local.start()
     local.wait()
 
@@ -295,16 +301,11 @@
         add_blocks(acc1, recv_a, o, o, 0, B, every)
         return 0
 
-    for i in range(bits - 1, -1, -1):
+    lax.fori_loop(1, Q, collect_near, 0)
+    for i in range(bits - 1, 0, -1):
         relay_copy(i).wait_recv()
         relay_copy(i).wait_send()
-        if i > 0:
-            relay_copy(i - 1).start()
-        if i == bits - 1:
-            lax.fori_loop(1, Q, collect_near, 0)
-    lax.fori_loop(1, Q, send_far_replies, 0)
-    for k in range(CAP):
-        recv_c[pair, k] = far_block(w, k)
+        relay_copy(i - 1).start()
     across.wait_recv()
     acc1[...] += half_recv[...].astype(f32)
 
@@ -327,7 +328,6 @@
 
     def free_a(d, _):
         near_copy(send_a, recv_a, a_s, a_r, d).wait_send()
-        far_copy(send_a, recv_a, a_s, a_r, d).wait_send()
         return 0
 
     lax.fori_loop(1, Q, free_a, 0)
@@ -351,6 +351,20 @@
     lax.fori_loop(1, W, send_terms2, 0)
     for k in range(CAP):
         recv_b[w, k] = term2(w, k)
+
+    relay_copy(0).wait_recv()
+    relay_copy(0).wait_send()
+    lax.fori_loop(1, Q, send_far_replies, 0)
+    for k in range(CAP):
+        recv_c[pair, k] = far_block(w, k)
+
+    def send_later(d, _):
+        user_copy(0, d).wait_send()
+        for c in range(1, C):
+            user_copy(c, d).start()
+        return 0
+
+    lax.fori_loop(1, W, send_later, 0)
 
     def wait_replies(d, _):
         for c in (near_copy(send_c, recv_c, c_s, c_r, d), far_copy(send_c, recv_c, c_s, c_r, d)):
@@ -376,32 +390,6 @@
 
     lax.fori_loop(0, T2, back, 0)
 
-    def send_later(d, _):
-        user_copy(0, d).wait_send()
-        for c in range(1, C):
-            user_copy(c, d).start()
-        return 0
-
-    lax.fori_loop(1, W, send_later, 0)
-
-    def finish(b, total):
-        m = mixed[b]
-        s = 1.0 / (1.0 + jnp.exp(-m))
-        gm = (gact[b] * s * (1.0 + m * (1.0 - s))).astype(bf16)
-        gb_out[b] = lax.dot_general(
-            gm, weight[...], (((1,), (1,)), ((), ())), preferred_element_type=f32
-        ).astype(bf16)
-        gw_out[...] += lax.dot_general(
-            emb[b], gm, (((0,), (0,)), ((), ())), preferred_element_type=f32
-        )
-        return total
-
-    gw_out[...] = jnp.zeros_like(gw_out)
-    lax.fori_loop(0, B, finish, 0)
-
-    for i in range(G):
-        gw_send[i] = gw_out[i * R:(i + 1) * R, :].astype(bf16)
-
     def group(d):
         return lax.rem(g + d, G)
 
@@ -433,9 +421,6 @@
             return 0
 
         lax.fori_loop(1, size, go, 0)
-
-    start_all(group_copy1, G)
-    gw_recv[g] = gw_send[g]
 
     def collect2(c):
         def go(d, _):
@@ -510,6 +495,28 @@
 
     lax.fori_loop(1, W, collect2(0), 0)
     narrow_step(0, 0)
+    def finish(b, total):
+        m = mixed[b]
+        s = 1.0 / (1.0 + jnp.exp(-m))
+        gm = (gact[b] * s * (1.0 + m * (1.0 - s))).astype(bf16)
+        gb_out[b] = lax.dot_general(
+            gm, weight[...], (((1,), (1,)), ((), ())), preferred_element_type=f32
+        ).astype(bf16)
+        gw_out[...] += lax.dot_general(
+            emb[b], gm, (((0,), (0,)), ((), ())), preferred_element_type=f32
+        )
+        return total
+
+    gw_out[...] = jnp.zeros_like(gw_out)
+    lax.fori_loop(0, B, finish, 0)
+
+    for i in range(G):
+        gw_send[i] = gw_out[i * R:(i + 1) * R, :].astype(bf16)
+
+    start_all(group_copy1, G)
+    gw_recv[g] = gw_send[g]
+    steps = 2 * bits
+    narrow_step(0, 1)
     wait_all(group_copy1, G)
     part = gw_recv[0].astype(f32)
     for i in range(1, G):
@@ -517,11 +524,11 @@
     gw_part[...] = part
     gw_parts[h * N + n] = part
     start_all(cross_copy, H * N)
-    steps = 2 * bits
     for c in range(1, C):
         for step in range(1, steps + 1):
-            narrow_step(c - 1, step)
-            if step == 1 and c == 1:
+            if step > 1 or c > 1:
+                narrow_step(c - 1, step)
+            if step == 2 and c == 1:
                 wait_all(cross_copy, H * N)
                 part = gw_parts[0]
                 for i in range(1, H * N):
@@ -546,6 +553,16 @@
     wait_all(group_copy3, G)
     for i in range(G):
         gw_out[i * R:(i + 1) * R, :] = gw_fin[i].astype(f32)
+
+
+def place_kernel(a, b, c, x, y, z, sems):
+    copies = [pltpu.make_async_copy(src, dst, sems.at[i]) for i, (src, dst) in enumerate(
+        [(a, x), (b, y), (c, z)]
+    )]
+    for copy in copies:
+        copy.start()
+    for copy in copies:
+        copy.wait()
 
 
 def local(
@@ -584,7 +601,7 @@
         scratch_shapes=[
             pltpu.VMEM((W, 8, 128), jnp.int32),
             pltpu.VMEM((W, 8, 128), jnp.int32),
-            pltpu.SMEM((W, 8, 128), jnp.int32),
+            pltpu.SMEM((W, 1, 128), jnp.int32),
             pltpu.VMEM(slots, bf16),
             pltpu.VMEM(slots, bf16),
             pltpu.VMEM(slots, bf16),
@@ -624,6 +641,15 @@
         bundle_degree.reshape(B, 1, TILE), user_degree.reshape(U, 1, TILE),
         cotangent.reshape(U, TILE, F),
     )
+    hbm = pl.BlockSpec(memory_space=pl.ANY)
+    uout, gw, gb = pl.pallas_call(
+        place_kernel,
+        out_shape=tuple(jax.ShapeDtypeStruct(x.shape, x.dtype) for x in (uout, gw, gb)),
+        in_specs=[hbm] * 3,
+        out_specs=(hbm,) * 3,
+        scratch_shapes=[dma((3,))],
+        name="place",
+    )(uout, gw, gb)
     return uout.reshape(U * TILE, F), gw, gb.reshape(B * TILE, F)
 
 

time: 96.6 us -> 140 us (1.45)
  Pallas kernels: 90.9 us -> 139 us
  local copies, waits for them, and re-layouts: 4.05 us -> 0 us
    pallas_call x0 -> x1, Pallas kernels: none -> 48.8 us  [local(): pl.pallas_call(place_kernel, out_shape=tuple((jax.ShapeDtypeStruct(x.shap...]
    unnamed x7 -> x0, local copies, waits for them, and re-layouts: 4.05 us -> none
where the time goes in v3:
time: 140 us
  Pallas kernels  139 us (99%)
    pallas_call x1, Pallas kernels, local(): pl.pallas_call(functools.partial(main_kernel, W, N, G, B, U, T2), out_sha...  88.5 us
    pallas_call x1, Pallas kernels, local(): pl.pallas_call(place_kernel, out_shape=tuple((jax.ShapeDtypeStruct(x.shap...  48.8 us

profile of v3, /device:TPU:0, one launch (start us, length us, event | category | flops | bytes accessed | tf_op | source)
XLA Modules:
  0.0 139.7 jit_solution(8910556268399996588)
XLA Ops:
  0.6 1.8 %plan.1.table = s32[76]{0:T(128)} custom-call(s32[12]{0:T(128)} %bitcast.12, s32[12]{0:T(128)} %slot1.1, s32[12]{0:T(128)} %bitcast.13, s32[12]{0:T(128)} %slot2.1), custom_call_target="tpu_custom_call" | custom-call | tf_op jit(solution)/shard_map/plan/pallas_call | solution.py:581
  2.4 88.5 %hypergraph.1 = (bf16[16,128,256]{2,1,0:T(8,128)(2,1)}, f32[256,256]{1,0:T(8,128)}, bf16[4,128,256]{2,1,0:T(8,128)(2,1)}) custom-call(s32[76]{0:T(128)} %plan.1.table, s32[12]{0:T(128)} %source1.1, s32[12]{0:T(128)} %source2.1, bf16[4,128,256]{2,1,0:T(8,128)(2,1)} %bitcast.9, bf16[12,128,128]{2,1,0:T(8,128)(2,1)} %tile1.1, bf16[12,128,128]{2,1,0:T(8,128)(2,1)} %tile2.1, ...), custom_call_target="tpu_custom_call" | custom-call | tf_op jit(solution)/shard_map/hypergraph/pallas_call | solution.py:592
  90.9 48.8 %place.1 = (bf16[16,128,256]{2,1,0:T(8,128)(2,1)}, f32[256,256]{1,0:T(8,128)}, bf16[4,128,256]{2,1,0:T(8,128)(2,1)}) custom-call(bf16[16,128,256]{2,1,0:T(8,128)(2,1)} %get-tuple-element.9.a, f32[256,256]{1,0:T(8,128)} %get-tuple-element.10.b, bf16[4,128,256]{2,1,0:T(8,128)(2,1)} %get-tuple-element.11.c), custom_call_target="tpu_custom_call" | custom-call | tf_op jit(solution)/shard_map/place/pallas_call | solution.py:645

commit v4 on v3

--- a/solution.py
+++ b/solution.py
@@ -59,11 +59,11 @@
     W, N, G, B, U, T2,
     table, source1, source2,
     items, tile1, tile2, weight, bdeg, udeg, cot,
-    uout, gw_out, gb_out,
+    users, gw_fin, gb_out,
     labs, rlab, slab,
     send_a, send_c, recv_a, recv_b, recv_c,
     inv_u, scaled, relay, half_send, half_recv, acc1, gact, emb, mixed, act, acc2,
-    gw_send, gw_recv, gw_part, gw_parts, gw_fin,
+    gw_out, gw_send, gw_recv, gw_part, gw_parts,
     red_send, red_recv,
     lab_s, lab_r, copy_sem, a_s, a_r, b_s, b_r, c_s, c_r,
     g1_s, g1_r, g2_s, g2_r, g3_s, g3_r, n_s, n_r, r_s, r_r, h_s, h_r,
@@ -191,24 +191,28 @@
         t = table[o * CAP + k]
         return jnp.dot(tile1[t], items[source1[t]], preferred_element_type=f32).astype(bf16)
 
+    def put(buffer, o, k, value):
+        for c in range(C):
+            buffer[o, c, k] = value[:, c * TILE:(c + 1) * TILE]
+
     def send_far1(d, _):
         o = far(mate(d))
         for k in range(CAP):
-            send_a[o, k] = term1(o, k)
+            put(send_a, o, k, term1(o, k))
         far_copy(send_a, recv_a, a_s, a_r, d).start()
         return 0
 
     def make_near1(d, _):
         o = mate(d)
         for k in range(CAP):
-            send_a[o, k] = term1(o, k)
+            put(send_a, o, k, term1(o, k))
         return 0
 
     lax.fori_loop(1, Q, send_far1, 0)
     lax.fori_loop(1, Q, make_near1, 0)
     for k in range(CAP):
-        recv_a[pair, k] = term1(pair, k)
-        recv_a[w, k] = term1(w, k)
+        put(recv_a, pair, k, term1(pair, k))
+        put(recv_a, w, k, term1(w, k))
     lax.fori_loop(size, U, scale_rest, 0)
 
     def release_near1(d, _):
@@ -231,29 +235,30 @@
 
     ROWS = 32
 
-    def add_blocks(acc, recv, place, o, column, blocks, cols):
-        labels = [slab[o, 0, column + k] for k in range(CAP)]
+    def add_blocks(acc, recv, place, o, start, blocks, columns=range(C)):
+        labels = [slab[o, 0, start + k] for k in range(CAP)]
 
         def part(r, _):
             rows = pl.ds(pl.multiple_of(r * ROWS, ROWS), ROWS)
-            xs = [recv[place, k, rows, cols].astype(f32) for k in range(CAP)]
-            for b in range(blocks):
-                total = acc[b, rows, cols]
-                for k in range(CAP):
-                    total = total + xs[k] * (labels[k] == b).astype(f32)
-                acc[b, rows, cols] = total
+            for c in columns:
+                cols = slice(c * TILE, (c + 1) * TILE)
+                xs = [recv[place, c, k, rows, :].astype(f32) for k in range(CAP)]
+                for b in range(blocks):
+                    total = acc[b, rows, cols]
+                    for k in range(CAP):
+                        total = total + xs[k] * (labels[k] == b).astype(f32)
+                    acc[b, rows, cols] = total
             return 0
 
         lax.fori_loop(0, TILE // ROWS, part, 0)
 
-    every = slice(0, F)
     gact[...] = jnp.zeros_like(gact)
-    add_blocks(gact, recv_a, pair, w, 2 * CAP, B, every)
+    add_blocks(gact, recv_a, pair, w, 2 * CAP, B)
 
     def collect_far(d, _):
         far_copy(send_a, recv_a, a_s, a_r, d).wait_recv()
         o = mate_back(d)
-        add_blocks(gact, recv_a, far(o), o, 2 * CAP, B, every)
+        add_blocks(gact, recv_a, far(o), o, 2 * CAP, B)
         return 0
 
     lax.fori_loop(1, Q, collect_far, 0)
@@ -293,12 +298,12 @@
         recv_c[w, k] = near_block(w, k)
 
     acc1[...] = jnp.zeros_like(acc1)
-    add_blocks(acc1, recv_a, w, w, 0, B, every)
+    add_blocks(acc1, recv_a, w, w, 0, B)
 
     def collect_near(d, _):
         near_copy(send_a, recv_a, a_s, a_r, d).wait_recv()
         o = mate_back(d)
-        add_blocks(acc1, recv_a, o, o, 0, B, every)
+        add_blocks(acc1, recv_a, o, o, 0, B)
         return 0
 
     lax.fori_loop(1, Q, collect_near, 0)
@@ -337,20 +342,20 @@
 
     def user_copy(c, d):
         return remote(
-            send_a.at[up(d), :, :, column(c)], recv_b.at[w, :, :, column(c)],
+            send_a.at[up(d), c], recv_b.at[w, c],
             b_s.at[c, d], b_r.at[c, d], (up(d), n),
         )
 
     def send_terms2(d, _):
         o = up(d)
         for k in range(CAP):
-            send_a[o, k] = term2(o, k)
+            put(send_a, o, k, term2(o, k))
         user_copy(0, d).start()
         return 0
 
     lax.fori_loop(1, W, send_terms2, 0)
     for k in range(CAP):
-        recv_b[w, k] = term2(w, k)
+        put(recv_b, w, k, term2(w, k))
 
     relay_copy(0).wait_recv()
     relay_copy(0).wait_send()
@@ -373,7 +378,7 @@
         return 0
 
     acc2[...] = jnp.zeros_like(acc2)
-    add_blocks(acc2, recv_b, w, w, CAP, U, every)
+    add_blocks(acc2, recv_b, w, w, CAP, U)
     gact[...] = jnp.zeros_like(gact)
     lax.fori_loop(1, Q, wait_replies, 0)
 
@@ -425,7 +430,7 @@
     def collect2(c):
         def go(d, _):
             user_copy(c, d).wait_recv()
-            add_blocks(acc2, recv_b, down(d), down(d), CAP, U, column(c))
+            add_blocks(acc2, recv_b, down(d), down(d), CAP, U, [c])
             return 0
 
         return go
@@ -439,7 +444,7 @@
 
     def double_copy(c, i):
         mine, _, many, peer = spans[i]
-        span = uout.at[pl.ds(mine, many), :, column(c)]
+        span = users.at[c, pl.ds(mine, many)]
         return remote(span, span, n_s.at[c, bits + i], n_r.at[c, bits + i], (w, peer))
 
     def halve_start(c, i):
@@ -467,7 +472,7 @@
     def divide(c):
         def go(j, _):
             b = base + j
-            uout[b, :, column(c)] = (acc2[b, :, column(c)] * inv_u[b]).astype(bf16)
+            users[c, b] = (acc2[b, :, column(c)] * inv_u[b]).astype(bf16)
             return 0
 
         lax.fori_loop(0, size, go, 0)
@@ -551,18 +556,21 @@
     across.wait_send()
     lax.fori_loop(1, W, free_b, 0)
     wait_all(group_copy3, G)
-    for i in range(G):
-        gw_out[i * R:(i + 1) * R, :] = gw_fin[i].astype(f32)
-
-
-def place_kernel(a, b, c, x, y, z, sems):
-    copies = [pltpu.make_async_copy(src, dst, sems.at[i]) for i, (src, dst) in enumerate(
-        [(a, x), (b, y), (c, z)]
-    )]
-    for copy in copies:
-        copy.start()
-    for copy in copies:
-        copy.wait()
+
+
+def place_kernel(users, gw, gb, x, y, z):
+    columns, blocks = users.shape[0], users.shape[1]
+    rows = gw.shape[1]
+
+    def block(b, _):
+        for c in range(columns):
+            x[b, :, c * TILE:(c + 1) * TILE] = users[c, b]
+        return 0
+
+    lax.fori_loop(0, blocks, block, 0)
+    for i in range(gw.shape[0]):
+        y[i * rows:(i + 1) * rows, :] = gw[i].astype(f32)
+    z[...] = gb[...]
 
 
 def local(
@@ -589,11 +597,12 @@
     dma = pltpu.SemaphoreType.DMA
     bits = N.bit_length() - 1
     slots = (W, CAP, TILE, F)
-    uout, gw, gb = pl.pallas_call(
+    halves = (W, F // TILE, CAP, TILE, TILE)
+    users, gw, gb = pl.pallas_call(
         functools.partial(main_kernel, W, N, G, B, U, T2),
         out_shape=(
-            jax.ShapeDtypeStruct((U, TILE, F), bf16),
-            jax.ShapeDtypeStruct((F, F), f32),
+            jax.ShapeDtypeStruct((F // TILE, U, TILE, TILE), bf16),
+            jax.ShapeDtypeStruct((G, R, F), bf16),
             jax.ShapeDtypeStruct((B, TILE, F), bf16),
         ),
         in_specs=[smem] * 3 + [vmem] * 7,
@@ -602,10 +611,10 @@
             pltpu.VMEM((W, 8, 128), jnp.int32),
             pltpu.VMEM((W, 8, 128), jnp.int32),
             pltpu.SMEM((W, 1, 128), jnp.int32),
+            pltpu.VMEM(halves, bf16),
             pltpu.VMEM(slots, bf16),
-            pltpu.VMEM(slots, bf16),
-            pltpu.VMEM(slots, bf16),
-            pltpu.VMEM(slots, bf16),
+            pltpu.VMEM(halves, bf16),
+            pltpu.VMEM(halves, bf16),
             pltpu.VMEM(slots, bf16),
             pltpu.VMEM((U, TILE, TILE), f32),
             pltpu.VMEM((U, TILE, F), bf16),
@@ -618,11 +627,11 @@
             pltpu.VMEM((B, TILE, F), f32),
             pltpu.VMEM((B, TILE, F), bf16),
             pltpu.VMEM((U, TILE, F), f32),
+            pltpu.VMEM((F, F), f32),
             pltpu.VMEM((G, R, F), bf16),
             pltpu.VMEM((G, R, F), bf16),
             pltpu.VMEM((R, F), f32),
             pltpu.VMEM((H * N, R, F), f32),
-            pltpu.VMEM((G, R, F), bf16),
             pltpu.VMEM((F // TILE, U, TILE, TILE), bf16),
             pltpu.VMEM((F // TILE, U, TILE, TILE), bf16),
             dma((W,)), dma((W,)), dma,
@@ -641,15 +650,17 @@
         bundle_degree.reshape(B, 1, TILE), user_degree.reshape(U, 1, TILE),
         cotangent.reshape(U, TILE, F),
     )
-    hbm = pl.BlockSpec(memory_space=pl.ANY)
     uout, gw, gb = pl.pallas_call(
         place_kernel,
-        out_shape=tuple(jax.ShapeDtypeStruct(x.shape, x.dtype) for x in (uout, gw, gb)),
-        in_specs=[hbm] * 3,
-        out_specs=(hbm,) * 3,
-        scratch_shapes=[dma((3,))],
+        out_shape=(
+            jax.ShapeDtypeStruct((U, TILE, F), bf16),
+            jax.ShapeDtypeStruct((F, F), f32),
+            jax.ShapeDtypeStruct((B, TILE, F), bf16),
+        ),
+        in_specs=[vmem] * 3,
+        out_specs=(vmem,) * 3,
         name="place",
-    )(uout, gw, gb)
+    )(users, gw, gb)
     return uout.reshape(U * TILE, F), gw, gb.reshape(B * TILE, F)
 
 

time: 140 us -> 94.3 us (0.67)
  Pallas kernels: 139 us -> 93 us
    pallas_call x1, Pallas kernels: 48.8 us -> 2.74 us  [local(): pl.pallas_call(place_kernel, out_shape=(jax.ShapeDtypeStruct((U, TILE, F)...]
where the time goes in v4:
time: 94.3 us; the launch traced here: 93.6 us
  Pallas kernels  93 us (99%)
    pallas_call x1, Pallas kernels, local(): pl.pallas_call(functools.partial(main_kernel, W, N, G, B, U, T2), out_sha...  88.5 us
    pallas_call x1, Pallas kernels, local(): pl.pallas_call(place_kernel, out_shape=(jax.ShapeDtypeStruct((U, TILE, F)...  2.74 us

profile of v4, /device:TPU:0, one launch (start us, length us, event | category | flops | bytes accessed | tf_op | source)
XLA Modules:
  0.0 93.6 jit_solution(8791925204431059610)
XLA Ops:
  0.6 1.8 %plan.1.table = s32[76]{0:T(128)} custom-call(s32[12]{0:T(128)} %bitcast.12, s32[12]{0:T(128)} %slot1.1, s32[12]{0:T(128)} %bitcast.13, s32[12]{0:T(128)} %slot2.1), custom_call_target="tpu_custom_call" | custom-call | tf_op jit(solution)/shard_map/plan/pallas_call | solution.py:589
  2.4 88.5 %hypergraph.1 = (bf16[2,16,128,128]{3,2,1,0:T(8,128)(2,1)}, bf16[8,32,256]{2,1,0:T(8,128)(2,1)}, bf16[4,128,256]{2,1,0:T(8,128)(2,1)}) custom-call(s32[76]{0:T(128)} %plan.1.table, s32[12]{0:T(128)} %source1.1, s32[12]{0:T(128)} %source2.1, bf16[4,128,256]{2,1,0:T(8,128)(2,1)} %bitcast.9, bf16[12,128,128]{2,1,0:T(8,128)(2,1)} %tile1.1, ...), custom_call_target="tpu_custom_call" | custom-call | tf_op jit(solution)/shard_map/hypergraph/pallas_call | solution.py:601
  90.9 2.7 %place.1 = (bf16[16,128,256]{2,1,0:T(8,128)(2,1)}, f32[256,256]{1,0:T(8,128)}, bf16[4,128,256]{2,1,0:T(8,128)(2,1)}) custom-call(bf16[2,16,128,128]{3,2,1,0:T(8,128)(2,1)} %get-tuple-element.9.users, bf16[8,32,256]{2,1,0:T(8,128)(2,1)} %get-tuple-element.10.gw, bf16[4,128,256]{2,1,0:T(8,128)(2,1)} %get-tuple-element.11.gb), custom_call_target="tpu_custom_call" | custom-call | tf_op jit(solution)/shard_map/place/pallas_call | solution.py:653

commit v5 on v4

--- a/solution.py
+++ b/solution.py
@@ -379,21 +379,6 @@
 
     acc2[...] = jnp.zeros_like(acc2)
     add_blocks(acc2, recv_b, w, w, CAP, U)
-    gact[...] = jnp.zeros_like(gact)
-    lax.fori_loop(1, Q, wait_replies, 0)
-
-    def back(t, _):
-        place = table[4 * SZ + t]
-        block = recv_c[place // CAP, place % CAP]
-        x = lax.dot_general(
-            tile2[t], block, (((0,), (0,)), ((), ())), preferred_element_type=f32
-        )
-        x = x.astype(bf16).astype(f32)
-        for b in range(B):
-            gact[b] += x * (source2[t] == b).astype(f32)
-        return 0
-
-    lax.fori_loop(0, T2, back, 0)
 
     def group(d):
         return lax.rem(g + d, G)
@@ -500,6 +485,23 @@
 
     lax.fori_loop(1, W, collect2(0), 0)
     narrow_step(0, 0)
+
+    gact[...] = jnp.zeros_like(gact)
+    lax.fori_loop(1, Q, wait_replies, 0)
+
+    def back(t, _):
+        place = table[4 * SZ + t]
+        block = recv_c[place // CAP, place % CAP]
+        x = lax.dot_general(
+            tile2[t], block, (((0,), (0,)), ((), ())), preferred_element_type=f32
+        )
+        x = x.astype(bf16).astype(f32)
+        for b in range(B):
+            gact[b] += x * (source2[t] == b).astype(f32)
+        return 0
+
+    lax.fori_loop(0, T2, back, 0)
+    narrow_step(0, 1)
     def finish(b, total):
         m = mixed[b]
         s = 1.0 / (1.0 + jnp.exp(-m))
@@ -521,7 +523,7 @@
     start_all(group_copy1, G)
     gw_recv[g] = gw_send[g]
     steps = 2 * bits
-    narrow_step(0, 1)
+    narrow_step(0, 2)
     wait_all(group_copy1, G)
     part = gw_recv[0].astype(f32)
     for i in range(1, G):
@@ -531,9 +533,9 @@
     start_all(cross_copy, H * N)
     for c in range(1, C):
         for step in range(1, steps + 1):
-            if step > 1 or c > 1:
+            if step > 2 or c > 1:
                 narrow_step(c - 1, step)
-            if step == 2 and c == 1:
+            if step == 3 and c == 1:
                 wait_all(cross_copy, H * N)
                 part = gw_parts[0]
                 for i in range(1, H * N):

time: 94.3 us -> 91.4 us (0.969)
  Pallas kernels: 93 us -> 89.5 us
    pallas_call x1, Pallas kernels: 88.5 us -> 85 us  [local(): pl.pallas_call(functools.partial(main_kernel, W, N, G, B, U, T2), out_sha...]
where the time goes in v5:
time: 91.4 us; the launch traced here: 90.1 us
  Pallas kernels  89.5 us (98%)
    pallas_call x1, Pallas kernels, local(): pl.pallas_call(functools.partial(main_kernel, W, N, G, B, U, T2), out_sha...  85 us
    pallas_call x1, Pallas kernels, local(): pl.pallas_call(place_kernel, out_shape=(jax.ShapeDtypeStruct((U, TILE, F)...  2.74 us

profile of v5, /device:TPU:0, one launch (start us, length us, event | category | flops | bytes accessed | tf_op | source)
XLA Modules:
  0.0 90.1 jit_solution(13850877578045092804)
XLA Ops:
  0.6 1.8 %plan.1.table = s32[76]{0:T(128)} custom-call(s32[12]{0:T(128)} %bitcast.12, s32[12]{0:T(128)} %slot1.1, s32[12]{0:T(128)} %bitcast.13, s32[12]{0:T(128)} %slot2.1), custom_call_target="tpu_custom_call" | custom-call | tf_op jit(solution)/shard_map/plan/pallas_call | solution.py:591
  2.4 85.0 %hypergraph.1 = (bf16[2,16,128,128]{3,2,1,0:T(8,128)(2,1)}, bf16[8,32,256]{2,1,0:T(8,128)(2,1)}, bf16[4,128,256]{2,1,0:T(8,128)(2,1)}) custom-call(s32[76]{0:T(128)} %plan.1.table, s32[12]{0:T(128)} %source1.1, s32[12]{0:T(128)} %source2.1, bf16[4,128,256]{2,1,0:T(8,128)(2,1)} %bitcast.9, bf16[12,128,128]{2,1,0:T(8,128)(2,1)} %tile1.1, ...), custom_call_target="tpu_custom_call" | custom-call | tf_op jit(solution)/shard_map/hypergraph/pallas_call | solution.py:603
  87.4 2.7 %place.1 = (bf16[16,128,256]{2,1,0:T(8,128)(2,1)}, f32[256,256]{1,0:T(8,128)}, bf16[4,128,256]{2,1,0:T(8,128)(2,1)}) custom-call(bf16[2,16,128,128]{3,2,1,0:T(8,128)(2,1)} %get-tuple-element.9.users, bf16[8,32,256]{2,1,0:T(8,128)(2,1)} %get-tuple-element.10.gw, bf16[4,128,256]{2,1,0:T(8,128)(2,1)} %get-tuple-element.11.gb), custom_call_target="tpu_custom_call" | custom-call | tf_op jit(solution)/shard_map/place/pallas_call | solution.py:655

commit v6 on v5

--- a/solution.py
+++ b/solution.py
@@ -166,49 +166,49 @@
         scale(lax.rem(base + j, U))
         return 0
 
+
+    def mate(d):
+        return side * Q + lax.rem(place_in + d, Q)
+
+    def mate_back(d):
+        return side * Q + lax.rem(place_in - d + Q, Q)
+
+    def far(o):
+        return lax.rem(o + Q, W)
+
+    def near_copy(src, dst, ss, rs, d):
+        return remote(src.at[mate(d)], dst.at[w], ss.at[d], rs.at[d], (mate(d), n))
+
+    def far_copy(src, dst, ss, rs, d):
+        return remote(src.at[far(mate(d))], dst.at[pair], ss.at[Q + d], rs.at[Q + d], (mate(d), n))
+
+    def term1(o, k):
+        t = table[o * CAP + k]
+        return jnp.dot(tile1[t], items[source1[t]], preferred_element_type=f32).astype(bf16)
+
+    def put(buffer, o, k, value):
+        for c in range(C):
+            buffer[o, c, k] = value[:, c * TILE:(c + 1) * TILE]
+
+    def send_far1(d, _):
+        o = far(mate(d))
+        for k in range(CAP):
+            put(send_a, o, k, term1(o, k))
+        far_copy(send_a, recv_a, a_s, a_r, d).start()
+        return 0
+
+    def make_near1(d, _):
+        o = mate(d)
+        for k in range(CAP):
+            put(send_a, o, k, term1(o, k))
+        return 0
+
+    lax.fori_loop(1, Q, send_far1, 0)
     lax.fori_loop(0, size, scale_first, 0)
     over = remote(
         scaled.at[pl.ds(base, size)], relay.at[pl.ds(base, size)], h_s.at[0], h_r.at[0], (pair, n)
     )
     over.start()
-
-    def mate(d):
-        return side * Q + lax.rem(place_in + d, Q)
-
-    def mate_back(d):
-        return side * Q + lax.rem(place_in - d + Q, Q)
-
-    def far(o):
-        return lax.rem(o + Q, W)
-
-    def near_copy(src, dst, ss, rs, d):
-        return remote(src.at[mate(d)], dst.at[w], ss.at[d], rs.at[d], (mate(d), n))
-
-    def far_copy(src, dst, ss, rs, d):
-        return remote(src.at[far(mate(d))], dst.at[pair], ss.at[Q + d], rs.at[Q + d], (mate(d), n))
-
-    def term1(o, k):
-        t = table[o * CAP + k]
-        return jnp.dot(tile1[t], items[source1[t]], preferred_element_type=f32).astype(bf16)
-
-    def put(buffer, o, k, value):
-        for c in range(C):
-            buffer[o, c, k] = value[:, c * TILE:(c + 1) * TILE]
-
-    def send_far1(d, _):
-        o = far(mate(d))
-        for k in range(CAP):
-            put(send_a, o, k, term1(o, k))
-        far_copy(send_a, recv_a, a_s, a_r, d).start()
-        return 0
-
-    def make_near1(d, _):
-        o = mate(d)
-        for k in range(CAP):
-            put(send_a, o, k, term1(o, k))
-        return 0
-
-    lax.fori_loop(1, Q, send_far1, 0)
     lax.fori_loop(1, Q, make_near1, 0)
     for k in range(CAP):
         put(recv_a, pair, k, term1(pair, k))

time: 91.4 us -> 89.4 us (0.978); the launches traced: 90.1 us -> 89.3 us
  no operation moved by 1% of the time
where the time goes in v6:
time: 89.4 us; the launch traced here: 89.3 us
  Pallas kernels  88.6 us (99%)
    pallas_call x1, Pallas kernels, local(): pl.pallas_call(functools.partial(main_kernel, W, N, G, B, U, T2), out_sha...  84.1 us
    pallas_call x1, Pallas kernels, local(): pl.pallas_call(place_kernel, out_shape=(jax.ShapeDtypeStruct((U, TILE, F)...  2.74 us

profile of v6, /device:TPU:0, one launch (start us, length us, event | category | flops | bytes accessed | tf_op | source)
XLA Modules:
  0.0 89.3 jit_solution(187117947300991582)
XLA Ops:
  0.6 1.8 %plan.1.table = s32[76]{0:T(128)} custom-call(s32[12]{0:T(128)} %bitcast.12, s32[12]{0:T(128)} %slot1.1, s32[12]{0:T(128)} %bitcast.13, s32[12]{0:T(128)} %slot2.1), custom_call_target="tpu_custom_call" | custom-call | tf_op jit(solution)/shard_map/plan/pallas_call | solution.py:591
  2.4 84.1 %hypergraph.1 = (bf16[2,16,128,128]{3,2,1,0:T(8,128)(2,1)}, bf16[8,32,256]{2,1,0:T(8,128)(2,1)}, bf16[4,128,256]{2,1,0:T(8,128)(2,1)}) custom-call(s32[76]{0:T(128)} %plan.1.table, s32[12]{0:T(128)} %source1.1, s32[12]{0:T(128)} %source2.1, bf16[4,128,256]{2,1,0:T(8,128)(2,1)} %bitcast.9, bf16[12,128,128]{2,1,0:T(8,128)(2,1)} %tile1.1, ...), custom_call_target="tpu_custom_call" | custom-call | tf_op jit(solution)/shard_map/hypergraph/pallas_call | solution.py:603
  86.5 2.7 %place.1 = (bf16[16,128,256]{2,1,0:T(8,128)(2,1)}, f32[256,256]{1,0:T(8,128)}, bf16[4,128,256]{2,1,0:T(8,128)(2,1)}) custom-call(bf16[2,16,128,128]{3,2,1,0:T(8,128)(2,1)} %get-tuple-element.9.users, bf16[8,32,256]{2,1,0:T(8,128)(2,1)} %get-tuple-element.10.gw, bf16[4,128,256]{2,1,0:T(8,128)(2,1)} %get-tuple-element.11.gb), custom_call_target="tpu_custom_call" | custom-call | tf_op jit(solution)/shard_map/place/pallas_call | solution.py:655
